TPU v7x, 128 devices: a whole 4x4x4 slice. The times are simulated.
128 devices in a mesh: tm: 4 (over x), sys: 32 (over z, y, core).
Axes of the slice: x: 4, y: 4, z: 4, core: 2. Of those that a mesh axis runs over, the one named last changes fastest.
Arguments:
- readings: float32 [8192, 16384], P('sys', 'tm'), may hold values from -20 to 60, as said below
- missing: int32 [8192, 16384], P('sys', 'tm'), may hold values 0 or 1
- left_init: float32 [8192, 64], P('sys'), may hold values from -6 to 6
- right_init: float32 [16384, 64], P('tm'), may hold values from -0.75 to 0.75
Outputs:
- left_factor: float32 [8192, 64], P('sys')
- right_factor: float32 [16384, 64], P('tm')
- sparse: float32 [8192, 16384], P('sys', 'tm')
- dual_var: float32 [8192, 16384], P('sys', 'tm')
Inputs may be any that keep to these rules, and one draw needn't show every extreme that they name: Power readings, rough from entry to entry.
All inputs are finite; a program needn't handle non-finite values. No bound on the sum of `missing` on one device may be relied on, other than what follows from the above.
Results may differ from a plain program's by a relative error of at most 0.0003.
Values sent between devices are 32-bit elements; how exact they have to be, the bound alone decides.
A program may use at most 64 MiB of HBM per device.

v0:
```python
import math

import jax
import jax.numpy as jnp
from jax import lax
from jax.sharding import PartitionSpec as P

ITERS = 2


def matmul_high(first_op, second_op):
    return jnp.dot(
        first_op, second_op, precision=lax.Precision.HIGHEST, preferred_element_type=jnp.float32
    )


def inner_rows(first_op, second_op):
    return lax.dot_general(
        first_op,
        second_op,
        (((0,), (0,)), ((), ())),
        precision=lax.Precision.HIGHEST,
        preferred_element_type=jnp.float32,
    )


def ridge_solve(factor, right_side):
    return jax.scipy.linalg.cho_solve((factor, True), right_side.T).T


def on_device(readings, missing, left_init, right_init):
    observed_mask = missing == 0
    total_count, abs_total = lax.psum(
        (
            jnp.sum(observed_mask.astype(jnp.float32)),
            jnp.sum(jnp.where(observed_mask, jnp.abs(readings), 0.0)),
        ),
        ("tm", "sys"),
    )
    penalty = total_count / (4.0 * abs_total + 1e-06)
    sys_rows = readings.shape[0]
    time_rows = readings.shape[1]
    sparsity_weight = 1.0 / math.sqrt(
        max(sys_rows * lax.axis_size("sys"), time_rows * lax.axis_size("tm"))
    )
    rank_width = left_init.shape[1]
    identity = jnp.eye(rank_width, dtype=jnp.float32)
    left_factor = left_init
    right_factor = right_init
    sparse = jnp.zeros_like(readings)
    dual_var = jnp.zeros_like(readings)
    for sweep in range(ITERS):
        low_rank = matmul_high(left_factor, right_factor.T)
        target = jnp.where(observed_mask, readings - sparse + dual_var / penalty, low_rank)
        gram_v = lax.psum(inner_rows(right_factor, right_factor), "tm") + identity
        left_sums = lax.psum(matmul_high(target, right_factor), "tm")
        left_factor = ridge_solve(jnp.linalg.cholesky(gram_v), left_sums)
        gram_u = lax.psum(inner_rows(left_factor, left_factor), "sys") + identity
        right_sums = lax.psum(inner_rows(target, left_factor), "sys")
        right_factor = ridge_solve(jnp.linalg.cholesky(gram_u), right_sums)
        low_rank = matmul_high(left_factor, right_factor.T)
        shifted = readings - low_rank + dual_var / penalty
        shrunk = jnp.sign(shifted) * jnp.maximum(jnp.abs(shifted) - sparsity_weight / penalty, 0.0)
        sparse = jnp.where(observed_mask, shrunk, 0.0)
        dual_var = jnp.where(
            observed_mask, dual_var + penalty * (readings - low_rank - sparse), 0.0
        )
        penalty = 1.5 * penalty
    return (left_factor, right_factor, sparse, dual_var)


def solution(mesh):
    in_specs = (P("sys", "tm"), P("sys", "tm"), P("sys", None), P("tm", None))
    out_specs = (P("sys", None), P("tm", None), P("sys", "tm"), P("sys", "tm"))
    return jax.shard_map(
        on_device, mesh=mesh, in_specs=in_specs, out_specs=out_specs, check_vma=False
    )
```

profile of v0, /device:TPU:0, one launch (start us, length us, event | category | flops | bytes accessed | tf_op | source)
XLA Modules:
  0.0 525.5 jit_solution(3689824887673832484)
XLA Ops:
  7.2 5.4 %convert_reduce_fusion = (f32[]{:T(128)}, f32[]{:T(128)}, pred[256,4096]{1,0:T(32,128)(4,1)S(1)}) fusion(f32[256,4096]{1,0:T(8,128)} %param.9, s32[256,4096]{1,0:T(8,128)} %param.10), kind=kLoop, calls=%fused_computation.7 | loop fusion | flops 6291454 | bytes 9437192 | tf_op jit(solution)/shard_map/reduce_sum | solution.py:35
  12.6 68.2 %all-reduce = (f32[]{:T(128)}, f32[]{:T(128)}) all-reduce(f32[]{:T(128)} %get-tuple-element.8, f32[]{:T(128)} %get-tuple-element.7), channel_id=1, replica_groups=mesh['tm'=4,'sys'=32] {'tm','sys'}, use_global_device_ids=true, to_apply=%region_4.6 | all-reduce | flops 2 | bytes 16 | tf_op jit(solution)/shard_map/psum | solution.py:33
  82.2 5.6 %convolution_select_fusion = f32[256,4096]{1,0:T(8,128)S(1)} fusion(pred[256,4096]{1,0:T(32,128)(4,1)S(1)} %get-tuple-element.13, f32[256,64]{0,1:T(8,128)S(1)} %copy-done.6, f32[4096,64]{0,1:T(8,128)S(1)} %copy-done, f32[256,4096]{1,0:T(8,128)} %param.9, f32[]{:T(128)S(6)} %div.32), kind=kOutput, calls=%fused_computation | convolution fusion | flops 807403520 | bytes 10551300 | tf_op jit(solution)/shard_map/dot_general | solution.py:12
  87.9 2.0 copy-done.1
  89.9 4.1 convolution_bitcast_fusion
  94.0 1.0 fusion.28
  95.0 15.6 %psum.70 = f32[64,64]{0,1:T(8,128)S(1)} all-reduce(f32[64,64]{0,1:T(8,128)S(1)} %fusion.28), channel_id=1, replica_groups=mesh['tm'=4,'sys'=32] {'tm'}, use_global_device_ids=true, to_apply=%region_0.0 | all-reduce | flops 4096 | bytes 32768 | tf_op jit(solution)/shard_map/psum | solution.py:55
  110.6 0.1 copy.9
  110.7 5.8 %cholesky.74 = f32[64,64]{1,0:T(8,128)S(1)} custom-call(f32[64,64]{1,0:T(8,128)S(1)} %fusion.23), custom_call_target="Cholesky" | custom-call | tf_op jit(solution)/shard_map/jit(cholesky)/cholesky | solution.py:57
  116.6 0.6 compare_reduce_fusion.3
  117.2 0.7 fusion
  118.6 4.9 custom-call.14
  124.2 7.3 %all-reduce.6.cloned.1.call-done = f32[64,256]{0,1:T(8,128)} async-done(((f32[64,256]{0,1:T(8,128)}), f32[64,256]{0,1:T(8,128)}) %all-reduce.6.cloned.1.call-update) | async-done | bytes 65552 | tf_op jit(solution)/shard_map/psum | solution.py:56
  131.6 1.2 fusion.21
  132.8 0.2 fusion.19
  133.0 5.8 %fusion.30 = f32[64,4096]{1,0:T(8,128)} fusion(f32[64,256]{1,0:T(8,128)S(1)} %fusion.19, f32[256,4096]{1,0:T(8,128)} %copy-done.1), kind=kOutput, calls=%fused_computation.63 | convolution fusion | flops 805306368 | bytes 5308416 | tf_op jit(solution)/shard_map/dot_general | solution.py:18
  138.7 0.2 fusion.29
  139.0 126.6 %psum.74 = f32[64,64]{0,1:T(8,128)S(1)} all-reduce(f32[64,64]{0,1:T(8,128)S(1)} %fusion.29), channel_id=1, replica_groups=mesh['tm'=4,'sys'=32] {'sys'}, use_global_device_ids=true, to_apply=%region_8.11 | all-reduce | flops 4096 | bytes 32768 | tf_op jit(solution)/shard_map/psum | solution.py:58
  265.6 0.1 copy.11
  265.7 5.8 %cholesky.85 = f32[64,64]{1,0:T(8,128)S(1)} custom-call(f32[64,64]{1,0:T(8,128)S(1)} %fusion.18), custom_call_target="Cholesky" | custom-call | tf_op jit(solution)/shard_map/jit(cholesky)/cholesky | solution.py:60
  271.6 0.6 compare_reduce_fusion.2
  272.2 0.7 fusion.1
  272.9 4.9 custom-call.15
  277.8 2.3 fusion.16
  280.1 1.0 fusion.14
  281.1 1.0 fusion.31
  282.1 16.0 %psum.76 = f32[64,64]{0,1:T(8,128)S(1)} all-reduce(f32[64,64]{0,1:T(8,128)S(1)} %fusion.31), channel_id=1, replica_groups=mesh['tm'=4,'sys'=32] {'tm'}, use_global_device_ids=true, to_apply=%region_10.14 | all-reduce | flops 4096 | bytes 32768 | tf_op jit(solution)/shard_map/psum | solution.py:55
  298.2 5.8 %cholesky.96 = f32[64,64]{1,0:T(8,128)S(1)} custom-call(f32[64,64]{1,0:T(8,128)S(1)} %fusion.13), custom_call_target="Cholesky" | custom-call | tf_op jit(solution)/shard_map/jit(cholesky)/cholesky | solution.py:57
  304.1 0.6 compare_reduce_fusion.1
  304.8 9.6 %add_select_fusion.1 = (f32[256,4096]{1,0:T(8,128)S(1)}, f32[256,4096]{1,0:T(8,128)}) fusion(pred[256,4096]{1,0:T(32,128)(4,1)S(1)} %get-tuple-element.13, f32[256,4096]{1,0:T(8,128)} %param.9, f32[]{:T(128)S(6)} %div.33, f32[]{:T(128)S(6)} %div.32, f32[]{:T(128)S(6)} %mul_shard_map.7, f32[]{:T(128)S(6)} %div.34, f32[64,256]{1,0:T(8,128)S(1)} %fusion.19, ...), kind=kOutput, calls=%fused_computation.4 | convolution fusion | flops 821035008 | bytes 14745616 | tf_op jit(solution)/shard_map/dot_general | solution.py:12
  314.3 2.0 copy-done.3
  316.3 4.6 fusion.32
  321.0 0.7 fusion.2
  321.6 4.9 custom-call.16
  326.5 30.0 %all-reduce.10.cloned.1.call-done = f32[64,256]{1,0:T(8,128)} async-done(((f32[64,256]{1,0:T(8,128)}), f32[64,256]{1,0:T(8,128)}) %all-reduce.10.cloned.1.call-update) | async-done | bytes 65552 | tf_op jit(solution)/shard_map/psum | solution.py:56
  356.6 1.1 fusion.11
  357.7 0.2 fusion.9
  357.9 5.8 %fusion.34 = f32[64,4096]{1,0:T(8,128)} fusion(f32[64,256]{1,0:T(8,128)S(1)} %fusion.9, f32[256,4096]{1,0:T(8,128)} %copy-done.3), kind=kOutput, calls=%fused_computation.67 | convolution fusion | flops 805306368 | bytes 5308416 | tf_op jit(solution)/shard_map/dot_general | solution.py:18
  363.7 0.2 fusion.33
  363.9 126.6 %psum.78 = f32[64,64]{0,1:T(8,128)S(1)} all-reduce(f32[64,64]{0,1:T(8,128)S(1)} %fusion.33), channel_id=1, replica_groups=mesh['tm'=4,'sys'=32] {'sys'}, use_global_device_ids=true, to_apply=%region_12.16 | all-reduce | flops 4096 | bytes 32768 | tf_op jit(solution)/shard_map/psum | solution.py:58
  490.5 0.1 copy.15
  490.6 5.8 %cholesky.107 = f32[64,64]{1,0:T(8,128)S(1)} custom-call(f32[64,64]{1,0:T(8,128)S(1)} %fusion.8), custom_call_target="Cholesky" | custom-call | tf_op jit(solution)/shard_map/jit(cholesky)/cholesky | solution.py:60
  496.5 0.6 compare_reduce_fusion
  497.1 0.7 fusion.3
  497.8 4.9 custom-call.17
  502.7 2.4 fusion.6
  505.1 1.0 fusion.4
  506.2 12.5 %add_select_fusion = (f32[256,4096]{1,0:T(8,128)}, f32[256,4096]{1,0:T(8,128)}) fusion(pred[256,4096]{1,0:T(32,128)(4,1)S(1)} %get-tuple-element.13, f32[]{:T(128)S(6)} %mul_shard_map.7, f32[]{:T(128)S(6)} %div.33, f32[]{:T(128)S(6)} %div.32, f32[256,4096]{1,0:T(8,128)S(1)} %copy-done.2, f32[256,4096]{1,0:T(8,128)} %get-tuple-element.15, f32[]{:T(128)S(6)} %div.34, ...), kind=kOutput, calls=%fused_computation.2 | convolution fusion | flops 830472192 | bytes 18939924 | tf_op jit(solution)/shard_map/dot_general | solution.py:12
  (35 shorter events, 0.6 us)
Async XLA Ops:
  7.2 75.0 %copy-start = (f32[4096,64]{0,1:T(8,128)S(1)}, f32[4096,64]{0,1:T(8,128)}, u32[]{:S(2)}) copy-start(f32[4096,64]{0,1:T(8,128)} %param.12) | copy-start | bytes 3145732
  7.2 75.0 %copy-start.6 = (f32[256,64]{0,1:T(8,128)S(1)}, f32[256,64]{0,1:T(8,128)}, u32[]{:S(2)}) copy-start(f32[256,64]{0,1:T(8,128)} %param.11) | copy-start | bytes 196612
  7.2 124.4 %all-reduce.6.cloned.1.call-start = ((), (), s32[]{:S(2)}) async-start(), calls=%async_computation | async-start | bytes 262144 | tf_op jit(solution)/shard_map/psum | solution.py:56
  87.9 2.0 copy-start.1
  94.0 183.8 %all-reduce.8.cloned.1.call-start = ((), (), s32[]{:S(2)}) async-start(), calls=%async_computation.1 | async-start | bytes 2097152 | tf_op jit(solution)/shard_map/psum | solution.py:59
  139.0 217.6 %all-reduce.10.cloned.1.call-start = ((), (), s32[]{:S(2)}) async-start(), calls=%async_computation.2 | async-start | bytes 131072 | tf_op jit(solution)/shard_map/psum | solution.py:56
  314.3 2.0 copy-start.3
  320.9 181.8 %all-reduce.12.cloned.1.call-start = ((), (), s32[]{:S(2)}) async-start(), calls=%async_computation.3 | async-start | bytes 2097152 | tf_op jit(solution)/shard_map/psum | solution.py:59
  357.9 148.3 %copy-start.5 = (f32[64,256]{1,0:T(8,128)}, f32[64,256]{1,0:T(8,128)S(1)}, u32[]{:S(2)}) copy-start(f32[64,256]{1,0:T(8,128)S(1)} %fusion.9) | copy-start | bytes 196612
  502.7 3.5 copy-start.2
  506.2 12.6 %copy-start.4 = (f32[64,4096]{1,0:T(8,128)}, f32[64,4096]{1,0:T(8,128)S(1)}, u32[]{:S(2)}) copy-start(f32[64,4096]{1,0:T(8,128)S(1)} %fusion.4) | copy-start | bytes 3145732
Sparse Core Ops, SparseCore 0:
  94.1 37.4 all-reduce.5
  139.1 105.5 all-reduce.7
  321.0 35.4 all-reduce.9
  364.0 105.5 all-reduce.11
where the time goes:
time: 532 us; the launch traced here: 525 us
  blocking collectives  353 us (66%)
  matrix products  59.6 us (11%)
  other arithmetic  53.8 us (10%)
  waiting for transfers between devices  37.5 us (7%)
  between operations  17 us (3%)
    psum x2, blocking collectives, on_device(): gram_u = lax.psum(inner_rows(left_factor, left_factor), 'sys') + identity  253 us
    psum x1, blocking collectives, on_device(): lax.psum((jnp.sum(observed_mask.astype(jnp.float32)), jnp.sum(jnp.where(o...  68.2 us
    psum x2, waiting for transfers between devices, on_device(): left_sums = lax.psum(matmul_high(target, right_factor), 'tm')  37.4 us
    dot_general x5, matrix products, matmul_high(): jnp.dot(first_op, second_op, precision=lax.Precision.HIGHEST, preferred_e...  36.3 us
    psum x2, blocking collectives, on_device(): gram_v = lax.psum(inner_rows(right_factor, right_factor), 'tm') + identity  31.7 us
    another operation x8, other arithmetic, ridge_solve(): return jax.scipy.linalg.cho_solve((factor, True), right_side.T).T  22.2 us
    dot_general x6, matrix products, inner_rows(): lax.dot_general(first_op, second_op, (((0,), (0,)), ((), ())), precision=...  13.9 us
    another operation x6, other arithmetic, on_device(): left_factor = ridge_solve(jnp.linalg.cholesky(gram_v), left_sums)  13 us
  transfers between devices with their start and end apart: 4, of which 2 were waited for; matrix products, arithmetic and copies ran while one was open for 8% of the time, Pallas kernels for 0%

commit v1 on v0

v1 whole, which is shorter than its diff:
```python
import functools
import math

import jax
import jax.numpy as jnp
from jax import lax
from jax.experimental import pallas as pl
from jax.experimental.pallas import tpu as pltpu
from jax.sharding import PartitionSpec as P

F32 = jnp.float32
BF16 = jnp.bfloat16
HIGH = lax.Precision.HIGHEST
MESH = pl.DeviceIdType.MESH
VMEM = pltpu.VMEM
RANK = 64
LANES = 128
ABSENT = 1e30
BLOCK = 512
MIB = 1 << 20


def split(value, parts):
    pieces = []
    for part in range(parts):
        piece = value.astype(BF16)
        pieces.append(piece)
        if part + 1 < parts:
            value = value - piece.astype(F32)
    return pieces


def dot(first_op, second_op):
    return jnp.dot(first_op, second_op, preferred_element_type=F32)


def dot_high(first_op, second_op):
    return jnp.dot(first_op, second_op, precision=HIGH, preferred_element_type=F32)


def dot_rows(first_op, second_op):
    return lax.dot_general(
        first_op, second_op, (((0,), (0,)), ((), ())), precision=HIGH, preferred_element_type=F32
    )


def dot_lanes(first_op, second_op, precision=None):
    return lax.dot_general(
        first_op,
        second_op,
        (((1,), (1,)), ((), ())),
        precision=precision,
        preferred_element_type=F32,
    )


def fold(wide):
    half = wide.shape[0] // 2
    return jnp.concatenate([wide[:half], wide[half:]], axis=1)


def unfold(packed):
    return jnp.concatenate([packed[:, :RANK], packed[:, RANK:]], axis=0)


def identity():
    row = lax.broadcasted_iota(jnp.int32, (RANK, RANK), 0)
    col = lax.broadcasted_iota(jnp.int32, (RANK, RANK), 1)
    return jnp.where(row == col, 1.0, 0.0).astype(F32)


def spd_inverse(gram):
    row = lax.broadcasted_iota(jnp.int32, (RANK, LANES), 0)

    def eliminate(_, both):
        cols = [jnp.broadcast_to(both[:, j : j + 1], (RANK, LANES)) for j in range(8)]
        for j in range(8):
            over = 1.0 / cols[j][j : j + 1, :]
            here = row == j
            pivot_row = both[j : j + 1, :] * over
            both = jnp.where(here, pivot_row, both - cols[j] * pivot_row)
            for later in range(j + 1, 8):
                entry = cols[later][j : j + 1, :] * over
                cols[later] = jnp.where(here, entry, cols[later] - cols[j] * entry)
        both = jnp.concatenate([both[8:], both[:8]], axis=0)
        return pltpu.roll(both, LANES - 8, 1)

    both = jnp.concatenate([gram, identity()], axis=1)
    return lax.fori_loop(0, RANK // 8, eliminate, both)[:, :RANK]


def threshold_of(sums, weight):
    count = jnp.sum(sums[0:1, :], axis=1, keepdims=True)
    total = jnp.sum(sums[1:2, :], axis=1, keepdims=True)
    penalty = count / (4.0 * total + 1e-06)
    return penalty, weight / penalty


def first_pass(readings, missing, left, right, seen, high, low_part, message, acc, gram, sums):
    step = pl.program_id(0)

    @pl.when(step == 0)
    def _():
        acc[...] = jnp.zeros_like(acc)
        gram[...] = jnp.zeros_like(gram)
        sums[...] = jnp.zeros_like(sums)

    left_a, left_b = split(left[...], 2)
    rows = right[...]
    right_a, right_b, right_c = split(rows, 3)
    low = dot_lanes(
        jnp.concatenate([left_a, left_a, left_b, left_b], axis=1),
        jnp.concatenate([right_a, right_b, right_a, right_b], axis=1),
    )
    observed = missing[...] == 0
    value = readings[...]
    seen[...] = jnp.where(observed, value, ABSENT)
    target = jnp.where(observed, value, low)
    target_a, target_b = split(target, 2)
    high[...] = target_a
    low_part[...] = target_b
    acc[...] += dot(target_a, jnp.concatenate([right_a, right_b, right_c], axis=1))
    acc[:, :LANES] += dot(target_b, jnp.concatenate([right_a, right_b], axis=1))
    gram[...] += dot_rows(rows, rows)
    count = jnp.sum(jnp.where(observed, 1.0, 0.0), axis=0, keepdims=True)
    total = jnp.sum(jnp.where(observed, jnp.abs(value), 0.0), axis=0, keepdims=True)
    for piece in range(BLOCK // LANES):
        at = slice(piece * LANES, (piece + 1) * LANES)
        sums[0:1, :] += count[:, at]
        sums[1:2, :] += total[:, at]

    @pl.when(step == pl.num_programs(0) - 1)
    def _():
        left_sums = acc[:, :RANK] + acc[:, RANK : 2 * RANK] + acc[:, 2 * RANK :]
        message[0:128, :] = fold(left_sums)
        message[128:160, :] = fold(gram[...])
        message[160:168, :] = sums[...]


def middle_pass(weight, seen, left, right, sums, clipped, scaled, message, acc, gram):
    step = pl.program_id(0)

    @pl.when(step == 0)
    def _():
        acc[...] = jnp.zeros_like(acc)
        gram[...] = jnp.zeros_like(gram)

    _, bound = threshold_of(sums[...], weight)
    left_a, left_b = split(left[...], 2)
    cols = jnp.concatenate([right[i] for i in range(BLOCK // LANES)], axis=1)
    right_a, right_b = split(cols, 2)
    low = dot(
        jnp.concatenate([left_a, left_a, left_b, left_b], axis=1),
        jnp.concatenate([right_a, right_b, right_a, right_b], axis=0),
    )
    value = seen[...]
    inside = jnp.maximum(jnp.minimum(value - low, bound), -bound)
    inside = jnp.where(value < 0.5 * ABSENT, inside, 0.0)
    clipped[...] = inside
    ratio = (inside * (1.0 / bound)).astype(BF16)
    scaled[...] = ratio
    acc[...] += dot_lanes(ratio, jnp.concatenate([right_a, right_b], axis=0))
    gram[...] += dot_lanes(cols, cols, HIGH)

    @pl.when(step == pl.num_programs(0) - 1)
    def _():
        left_sums = (acc[:, :RANK] + acc[:, RANK:]) * ((5.0 / 3.0) * bound)
        message[0:128, :] = fold(left_sums)
        message[128:160, :] = fold(gram[...])
        message[160:168, :] = jnp.zeros((8, LANES), F32)


def last_pass(weight, seen, clipped, left, right, sums, sparse, dual, right_out, left_out):
    penalty, bound = threshold_of(sums[...], weight)
    left_a, left_b = split(left[...], 2)
    cols = jnp.concatenate([right[i] for i in range(BLOCK // LANES)], axis=1)
    right_a, right_b = split(cols, 2)
    low = dot(
        jnp.concatenate([left_a, left_a, left_b, left_b], axis=1),
        jnp.concatenate([right_a, right_b, right_a, right_b], axis=0),
    )
    value = seen[...]
    present = value < 0.5 * ABSENT
    shifted = value - low + clipped[...] * (1.0 / 1.5)
    bound = bound / 1.5
    inside = jnp.maximum(jnp.minimum(shifted, bound), -bound)
    sparse[...] = jnp.where(present, shifted - inside, 0.0)
    dual[...] = jnp.where(present, inside * (1.5 * penalty), 0.0)
    right_out[...] = cols.T
    left_out[...] = left[...]


def exchange(first, weight, *refs):
    if first:
        message, high, low_part, left_out, right_out, sums_out = refs[:6]
        scratch = refs[6:]
    else:
        message, scaled, left_in, right_in, sums_in, left_out, right_out = refs[:7]
        scratch = refs[7:]
    (total, x_recv, gram_send, gram_core, gram_y, gram_z, partial, from_core, recv_a, recv_b, part_a,
     part_b, recv_a2, recv_b2, x_sems, g_sems, c_sems, s_sems, a_sems, f_sems) = scratch

    tm = lax.axis_index("tm")
    me = lax.axis_index("sys")
    core = me % 2
    y = (me // 2) % 4
    z = me // 8

    def at_sys(z_pos, y_pos, core_pos):
        return {"sys": (z_pos * 4 + y_pos) * 2 + core_pos}

    twin = at_sys(z, y, 1 - core)
    y_peer = [None] + [(y + k) % 4 for k in (1, 2, 3)]
    z_peer = [None] + [(z + k) % 4 for k in (1, 2, 3)]
    y_dev = [None] + [at_sys(z, y_peer[k], core) for k in (1, 2, 3)]
    z_dev = [None] + [at_sys(z_peer[k], y, core) for k in (1, 2, 3)]
    x_dev = [{"tm": tm + 1 - 2 * (tm % 2)}, {"tm": 3 - tm}]

    barrier = pltpu.get_barrier_semaphore()
    everyone = x_dev + [twin] + y_dev[1:] + z_dev[1:]
    for device in everyone:
        pl.semaphore_signal(barrier, inc=1, device_id=device, device_id_type=MESH)
    pl.semaphore_wait(barrier, len(everyone))

    def send(src, dst, sems, index, device):
        copy = pltpu.make_async_remote_copy(
            src_ref=src, dst_ref=dst, send_sem=sems.at[0, index], recv_sem=sems.at[1, index],
            device_id=device, device_id_type=MESH,
        )
        copy.start()
        return copy

    halves = (slice(0, 80), slice(80, 168))
    source = message
    for step in range(2):
        copies = [
            send(source.at[halves[h]], x_recv.at[step, halves[h]], x_sems, 2 * step + h, x_dev[(step + h) % 2])
            for h in range(2)
        ]
        for copy in copies:
            copy.wait()
        for h in range(2):
            total[step, halves[h]] = source[halves[h]] + x_recv[step, halves[h]]
        source = total.at[step]
    summed = total[1]
    left_sums = unfold(summed[0:128])
    inverse_v = spd_inverse(unfold(summed[128:160]) + identity())
    if first:
        left = dot_high(left_sums, inverse_v)
        beside = jnp.zeros((RANK, RANK), F32)
    else:
        before = left_in[...]
        left = before + dot_high(left_sums - before, inverse_v)
        beside = dot_rows(left, before)
    left_out[...] = left

    gram_send[0, 0:64, :] = jnp.concatenate([dot_rows(left, left), beside], axis=1)
    gram_send[0, 64:72, :] = summed[160:168]
    gram_copy = send(gram_send.at[0], gram_core, g_sems, 0, twin)

    left_a, left_b, left_c = split(left.T, 3)
    stacked_two = jnp.concatenate([left_a, left_b], axis=0)
    stacked_three = jnp.concatenate([left_a, left_b, left_c], axis=0)

    def products(half, group):
        at = pl.ds(pl.multiple_of(half * 2048 + group * BLOCK, BLOCK), BLOCK)
        if first:
            wide = dot(stacked_three, high[:, at])
            small = dot(stacked_two, low_part[:, at])
            value = wide[0:64] + (wide[64:128] + (wide[128:192] + (small[0:64] + small[64:128])))
        else:
            wide = dot(stacked_two, scaled[:, at])
            value = wide[0:64] + wide[64:128]
        for i in range(4):
            partial[half, group, i] = value[:, i * LANES : (i + 1) * LANES]

    core_copies = []
    for group in range(4):
        products(1 - core, group)
        core_copies.append(
            send(partial.at[1 - core, group], from_core.at[group], c_sems, group, twin)
        )
    for group in range(4):
        products(core, group)

    gram_copy.wait()
    gram_send[1] = gram_send[0] + gram_core[...]
    copies = [send(gram_send.at[1], gram_y.at[k - 1], g_sems, k, y_dev[k]) for k in (1, 2, 3)]
    for group in range(4):
        core_copies[group].wait()
        partial[core, group] += from_core[group]
    for copy in copies:
        copy.wait()
    gram_send[2] = gram_send[1] + gram_y[0] + (gram_y[1] + gram_y[2])
    copies = [send(gram_send.at[2], gram_z.at[k - 1], g_sems, 3 + k, z_dev[k]) for k in (1, 2, 3)]
    first_a = [
        send(partial.at[core, y_peer[k], :, 0:32], recv_a.at[k - 1], s_sems, k - 1, y_dev[k]) for k in (1, 2, 3)
    ]
    first_b = [
        send(partial.at[core, :, z_peer[k], 32:64], recv_b.at[k - 1], s_sems, 2 + k, z_dev[k]) for k in (1, 2, 3)
    ]
    for copy in copies:
        copy.wait()
    grams = gram_send[2] + gram_z[0] + (gram_z[1] + gram_z[2])
    inverse_u = spd_inverse(grams[0:64, 0:64] + identity())

    for copy in first_a:
        copy.wait()
    part_a[...] = partial[core, y, :, 0:32] + recv_a[0] + (recv_a[1] + recv_a[2])
    second = [send(part_a.at[z_peer[k]], recv_a2.at[k - 1], s_sems, 5 + k, z_dev[k]) for k in (1, 2, 3)]
    for copy in first_b:
        copy.wait()
    part_b[...] = partial[core, :, z, 32:64] + recv_b[0] + (recv_b[1] + recv_b[2])
    second += [send(part_b.at[y_peer[k]], recv_b2.at[k - 1], s_sems, 8 + k, y_dev[k]) for k in (1, 2, 3)]
    for copy in second:
        copy.wait()
    sums_a = part_a[z] + recv_a2[0] + (recv_a2[1] + recv_a2[2])
    sums_b = part_b[y] + recv_b2[0] + (recv_b2[1] + recv_b2[2])
    right_sums = jnp.concatenate([sums_a, sums_b], axis=0)
    if first:
        sums_out[...] = grams[64:72]
    else:
        _, bound = threshold_of(sums_in[...], weight)
        right_sums = right_sums * ((5.0 / 3.0) * bound) + dot_high(grams[0:64, 64:128], right_in[core, y, z])
    right_out[core, y, z] = dot_high(inverse_u, right_sums)

    mine = right_out.at[core, y, z]
    to_twin = [send(mine, mine, f_sems, 0, twin)]
    gather_a = [send(mine.at[0:32], mine.at[0:32], a_sems, k - 1, z_dev[k]) for k in (1, 2, 3)]
    gather_b = [send(mine.at[32:64], mine.at[32:64], a_sems, 2 + k, y_dev[k]) for k in (1, 2, 3)]
    for copy in gather_a:
        copy.wait()
    row_a = right_out.at[core, y, :, 0:32]
    last_a = [send(row_a, row_a, a_sems, 5 + k, y_dev[k]) for k in (1, 2, 3)]
    for copy in gather_b:
        copy.wait()
    row_b = right_out.at[core, :, z, 32:64]
    last_b = [send(row_b, row_b, a_sems, 8 + k, z_dev[k]) for k in (1, 2, 3)]
    for k in (1, 2, 3):
        here = right_out.at[core, y, (z + 4 - k) % 4, 0:32]
        to_twin.append(send(here, here, f_sems, k, twin))
        here = right_out.at[core, (y + 4 - k) % 4, z, 32:64]
        to_twin.append(send(here, here, f_sems, 3 + k, twin))
    for k in (1, 2, 3):
        last_a[k - 1].wait()
        here = right_out.at[core, (y + 4 - k) % 4, :, 0:32]
        to_twin.append(send(here, here, f_sems, 6 + k, twin))
        last_b[k - 1].wait()
        here = right_out.at[core, :, (z + 4 - k) % 4, 32:64]
        to_twin.append(send(here, here, f_sems, 9 + k, twin))
    for copy in to_twin:
        copy.wait()


def whole():
    return pl.BlockSpec(memory_space=VMEM)


def params(limit, **more):
    return pltpu.CompilerParams(vmem_limit_bytes=limit * MIB, **more)


def exchange_call(first, weight, *operands):
    dma = pltpu.SemaphoreType.DMA
    shapes = [
        jax.ShapeDtypeStruct((256, RANK), F32),
        jax.ShapeDtypeStruct((2, 4, 4, RANK, LANES), F32),
    ]
    if first:
        shapes.append(jax.ShapeDtypeStruct((8, LANES), F32))
    return pl.pallas_call(
        functools.partial(exchange, first, weight),
        out_shape=shapes,
        in_specs=[whole()] * len(operands),
        out_specs=[whole()] * len(shapes),
        scratch_shapes=[
            VMEM((2, 168, LANES), F32),
            VMEM((2, 168, LANES), F32),
            VMEM((3, 72, LANES), F32),
            VMEM((72, LANES), F32),
            VMEM((3, 72, LANES), F32),
            VMEM((3, 72, LANES), F32),
            VMEM((2, 4, 4, RANK, LANES), F32),
            VMEM((4, 4, RANK, LANES), F32),
            VMEM((3, 4, 32, LANES), F32),
            VMEM((3, 4, 32, LANES), F32),
            VMEM((4, 32, LANES), F32),
            VMEM((4, 32, LANES), F32),
            VMEM((3, 32, LANES), F32),
            VMEM((3, 32, LANES), F32),
            dma((2, 4)),
            dma((2, 7)),
            dma((2, 4)),
            dma((2, 12)),
            dma((2, 12)),
            dma((2, 13)),
        ],
        compiler_params=params(24, collective_id=0 if first else 1, has_side_effects=True),
        cost_estimate=pl.CostEstimate(flops=10**9, bytes_accessed=10**7, transcendentals=0),
    )(*operands)


def on_device(weight, readings, missing, left_init, right_init):
    rows, times = readings.shape
    steps = times // BLOCK
    tile = pl.BlockSpec((rows, BLOCK), lambda i: (0, i))
    fixed = lambda *shape: pl.BlockSpec(shape, lambda i: (0,) * len(shape))
    chunks = pl.BlockSpec((BLOCK // LANES, RANK, LANES), lambda i: (i, 0, 0))
    time_rows = pl.BlockSpec((BLOCK, RANK), lambda i: (i, 0))
    full = lambda kind: jax.ShapeDtypeStruct((rows, times), kind)
    message_shape = jax.ShapeDtypeStruct((168, LANES), F32)

    seen, high, low_part, message = pl.pallas_call(
        first_pass,
        grid=(steps,),
        out_shape=[full(F32), full(BF16), full(BF16), message_shape],
        in_specs=[tile, tile, fixed(rows, RANK), time_rows],
        out_specs=[tile, tile, tile, fixed(168, LANES)],
        scratch_shapes=[VMEM((rows, 3 * RANK), F32), VMEM((RANK, RANK), F32), VMEM((8, LANES), F32)],
        compiler_params=params(24),
    )(readings, missing, left_init, right_init)
    left, right, sums = exchange_call(True, weight, message, high, low_part)
    flat = lambda value: value.reshape(32, RANK, LANES)
    clipped, scaled, message = pl.pallas_call(
        functools.partial(middle_pass, weight),
        grid=(steps,),
        out_shape=[full(F32), full(BF16), message_shape],
        in_specs=[tile, fixed(rows, RANK), chunks, fixed(8, LANES)],
        out_specs=[tile, tile, fixed(168, LANES)],
        scratch_shapes=[VMEM((rows, 2 * RANK), F32), VMEM((RANK, RANK), F32)],
        compiler_params=params(24),
    )(seen, left, flat(right), sums)
    left, right = exchange_call(False, weight, message, scaled, left, right, sums)
    sparse, dual, right_factor, left_factor = pl.pallas_call(
        functools.partial(last_pass, weight),
        grid=(steps,),
        out_shape=[
            full(F32), full(F32), jax.ShapeDtypeStruct((times, RANK), F32),
            jax.ShapeDtypeStruct((rows, RANK), F32),
        ],
        in_specs=[tile, tile, fixed(rows, RANK), chunks, fixed(8, LANES)],
        out_specs=[tile, tile, time_rows, fixed(rows, RANK)],
        compiler_params=params(24),
    )(seen, clipped, left, flat(right), sums)
    return left_factor, right_factor, sparse, dual


def solution(mesh):
    weight = 1.0 / math.sqrt(max(8192, 16384))
    in_specs = (P("sys", "tm"), P("sys", "tm"), P("sys", None), P("tm", None))
    out_specs = (P("sys", None), P("tm", None), P("sys", "tm"), P("sys", "tm"))
    return jax.shard_map(
        functools.partial(on_device, weight), mesh=mesh, in_specs=in_specs, out_specs=out_specs, check_vma=False
    )
```

time: 532 us -> 113 us (0.21)
  blocking collectives: 353 us -> 0 us
  Pallas kernels: 0 us -> 102 us
  matrix products: 59.6 us -> 0 us
  other arithmetic: 53.8 us -> 0 us
  waiting for transfers between devices: 37.5 us -> 0 us
  between operations: 17 us -> 0.68 us
    psum x5 -> x0, blocking collectives: 353 us -> none  [the longest x2 253 us: on_device(): gram_u = lax.psum(inner_rows(left_factor, left_factor), 'sys') + identity]
    pallas_call x0 -> x5, Pallas kernels: none -> 102 us  [the longest x2 82.4 us: exchange_call(): pl.pallas_call(functools.partial(exchange, first, weight), out_shape=shap...]
    dot_general x11 -> x0, matrix products: 50.2 us -> none  [the longest x5 36.3 us: matmul_high(): jnp.dot(first_op, second_op, precision=lax.Precision.HIGHEST, preferred_e...]
    another operation x20 -> x0, other arithmetic: 48.3 us -> none  [the longest x8 22.2 us: ridge_solve(): return jax.scipy.linalg.cho_solve((factor, True), right_side.T).T]
    psum x4 -> x0, waiting for transfers between devices: 37.4 us -> none  [the longest x2 37.4 us: on_device(): left_sums = lax.psum(matmul_high(target, right_factor), 'tm')]
    another operation x8 -> x0, matrix products: 9.36 us -> none  [ridge_solve(): return jax.scipy.linalg.cho_solve((factor, True), right_side.T).T]
    reduce_sum x1 -> x0, other arithmetic: 5.38 us -> none  [on_device(): jnp.sum(observed_mask.astype(jnp.float32))]
    unnamed x14 -> x8, local copies, waits for them, and re-layouts: 4.05 us -> 9.4 us
  transfers between devices with their start and end apart: 4 -> 0, of which waited for: 2 -> 0; matrix products, arithmetic and copies ran while one was open for 8% -> 0% of each run, Pallas kernels for 0% -> 0%
where the time goes in v1:
time: 113 us; the launch traced here: 112 us
  Pallas kernels  102 us (90%)
  local copies, waits for them, and re-layouts  9.4 us (8%)
    pallas_call x2, Pallas kernels, exchange_call(): pl.pallas_call(functools.partial(exchange, first, weight), out_shape=shap...  82.4 us
    unnamed x8, local copies, waits for them, and re-layouts  9.4 us
    pallas_call x1, Pallas kernels, on_device(): pl.pallas_call(first_pass, grid=(steps,), out_shape=[full(F32), full(BF16...  7.45 us
    pallas_call x1, Pallas kernels, on_device(): pl.pallas_call(functools.partial(last_pass, weight), grid=(steps,), out_s...  6.18 us
    pallas_call x1, Pallas kernels, on_device(): pl.pallas_call(functools.partial(middle_pass, weight), grid=(steps,), out...  5.64 us

profile of v1, /device:TPU:0, one launch (start us, length us, event | category | flops | bytes accessed | tf_op | source)
XLA Modules:
  0.0 111.8 jit_solution(9151108627342116966)
XLA Ops:
  0.6 0.9 copy.8.left
  1.6 1.8 %copy.9.right = f32[4096,64]{1,0:T(8,128)S(1)} copy(f32[4096,64]{0,1:T(8,128)} %param.7) | data formatting | bytes 2097152 | tf_op args[3]
  3.4 0.0 copy-start
  3.4 2.2 %copy-done = f32[256,4096]{1,0:T(8,128)S(1)} copy-done((f32[256,4096]{1,0:T(8,128)S(1)}, f32[256,4096]{1,0:T(8,128)}, u32[]{:S(2)}) %copy-start) | copy-done | bytes 4194328
  5.6 0.0 copy-start.1
  5.6 2.2 %copy-done.1 = s32[256,4096]{1,0:T(8,128)S(1)} copy-done((s32[256,4096]{1,0:T(8,128)S(1)}, s32[256,4096]{1,0:T(8,128)}, u32[]{:S(2)}) %copy-start.1) | copy-done | bytes 4194328
  7.8 7.5 %shard_map.75 = (f32[256,4096]{1,0:T(8,128)S(1)}, bf16[256,4096]{1,0:T(8,128)(2,1)S(1)}, bf16[256,4096]{1,0:T(8,128)(2,1)S(1)}, f32[168,128]{1,0:T(8,128)S(1)}) custom-call(f32[256,4096]{1,0:T(8,128)S(1)} %copy-done, s32[256,4096]{1,0:T(8,128)S(1)} %copy-done.1, f32[256,64]{1,0:T(8,128)S(1)} %copy.8.left, f32[4096,64]{1,0:T(8,128)S(1)} %copy.9.right), custom_call_target="tpu_custom_call" | custom-call | tf_op jit(solution)/shard_map/pallas_call | solution.py:413
  15.2 43.0 %shard_map.76 = (f32[256,64]{1,0:T(8,128)S(1)}, f32[2,4,4,64,128]{4,3,2,1,0:T(8,128)S(1)}, f32[8,128]{1,0:T(8,128)S(1)}) custom-call(f32[168,128]{1,0:T(8,128)S(1)} %get-tuple-element.21.refs_0_, bf16[256,4096]{1,0:T(8,128)(2,1)S(1)} %get-tuple-element.22.refs_1_, bf16[256,4096]{1,0:T(8,128)(2,1)S(1)} %get-tuple-element.23.refs_2_), custom_call_target="tpu_custom_call" | custom-call | flops 1000000000 | bytes 10000000 | tf_op jit(solution)/shard_map/pallas_call | solution.py:371
  58.3 5.6 %shard_map.77 = (f32[256,4096]{1,0:T(8,128)S(1)}, bf16[256,4096]{1,0:T(8,128)(2,1)S(1)}, f32[168,128]{1,0:T(8,128)S(1)}) custom-call(f32[256,4096]{1,0:T(8,128)S(1)} %get-tuple-element.20.seen, f32[256,64]{1,0:T(8,128)S(1)} %get-tuple-element.24.left.refs_2_, f32[32,64,128]{2,1,0:T(8,128)S(1)} %bitcast.3, f32[8,128]{1,0:T(8,128)S(1)} %get-tuple-element.26.sums.refs_4_), custom_call_target="tpu_custom_call" | custom-call | tf_op jit(solution)/shard_map/pallas_call | solution.py:424
  63.9 39.4 %shard_map.78 = (f32[256,64]{1,0:T(8,128)S(1)}, f32[2,4,4,64,128]{4,3,2,1,0:T(8,128)S(1)}) custom-call(f32[168,128]{1,0:T(8,128)S(1)} %get-tuple-element.28.refs_0_, bf16[256,4096]{1,0:T(8,128)(2,1)S(1)} %get-tuple-element.29.refs_1_, f32[256,64]{1,0:T(8,128)S(1)} %get-tuple-element.24.left.refs_2_, f32[2,4,4,64,128]{4,3,2,1,0:T(8,128)S(1)} %get-tuple-element.25.refs_3_, ...), custom_call_target="tpu_custom_call" | custom-call | flops 1000000000 | bytes 10000000 | tf_op jit(solution)/shard_map/pallas_call | solution.py:371
  103.3 6.2 %shard_map.79 = (f32[256,4096]{1,0:T(8,128)}, f32[256,4096]{1,0:T(8,128)}, f32[4096,64]{1,0:T(8,128)S(1)}, f32[256,64]{1,0:T(8,128)S(1)}) custom-call(f32[256,4096]{1,0:T(8,128)S(1)} %get-tuple-element.20.seen, f32[256,4096]{1,0:T(8,128)S(1)} %get-tuple-element.27.clipped, f32[256,64]{1,0:T(8,128)S(1)} %get-tuple-element.30.left, ...), custom_call_target="tpu_custom_call" | custom-call | tf_op jit(solution)/shard_map/pallas_call | solution.py:434
  109.5 0.7 copy.10
  110.2 1.6 %copy.11 = f32[4096,64]{0,1:T(8,128)} copy(f32[4096,64]{1,0:T(8,128)S(1)} %get-tuple-element.37) | data formatting | bytes 2097152
Async XLA Ops:
  3.4 2.2 %copy-start = (f32[256,4096]{1,0:T(8,128)S(1)}, f32[256,4096]{1,0:T(8,128)}, u32[]{:S(2)}) copy-start(f32[256,4096]{1,0:T(8,128)} %readings.1) | copy-start | bytes 12582916
  5.6 2.2 %copy-start.1 = (s32[256,4096]{1,0:T(8,128)S(1)}, s32[256,4096]{1,0:T(8,128)}, u32[]{:S(2)}) copy-start(s32[256,4096]{1,0:T(8,128)} %missing.1) | copy-start | bytes 12582916

commit v2 on v0

v2 whole, which is shorter than its diff:
```python
import functools
import math

import jax
import jax.numpy as jnp
from jax import lax
from jax.experimental import pallas as pl
from jax.experimental.pallas import tpu as pltpu
from jax.sharding import PartitionSpec as P

F32 = jnp.float32
BF16 = jnp.bfloat16
HIGH = lax.Precision.HIGHEST
MESH = pl.DeviceIdType.MESH
VMEM = pltpu.VMEM
RANK = 64
LANES = 128
ABSENT = 1e30
BLOCK = 512
MIB = 1 << 20


def split(value, parts):
    pieces = []
    for part in range(parts):
        piece = value.astype(BF16)
        pieces.append(piece)
        if part + 1 < parts:
            value = value - piece.astype(F32)
    return pieces


def dot(first_op, second_op):
    return jnp.dot(first_op, second_op, preferred_element_type=F32)


def dot_high(first_op, second_op):
    return jnp.dot(first_op, second_op, precision=HIGH, preferred_element_type=F32)


def dot_rows(first_op, second_op):
    return lax.dot_general(
        first_op, second_op, (((0,), (0,)), ((), ())), precision=HIGH, preferred_element_type=F32
    )


def dot_lanes(first_op, second_op, precision=None):
    return lax.dot_general(
        first_op,
        second_op,
        (((1,), (1,)), ((), ())),
        precision=precision,
        preferred_element_type=F32,
    )


def fold(wide):
    half = wide.shape[0] // 2
    return jnp.concatenate([wide[:half], wide[half:]], axis=1)


def unfold(packed):
    return jnp.concatenate([packed[:, :RANK], packed[:, RANK:]], axis=0)


def identity():
    row = lax.broadcasted_iota(jnp.int32, (RANK, RANK), 0)
    col = lax.broadcasted_iota(jnp.int32, (RANK, RANK), 1)
    return jnp.where(row == col, 1.0, 0.0).astype(F32)


def spd_inverse(gram):
    row = lax.broadcasted_iota(jnp.int32, (RANK, LANES), 0)

    def eliminate(_, both):
        cols = [jnp.broadcast_to(both[:, j : j + 1], (RANK, LANES)) for j in range(8)]
        for j in range(8):
            over = 1.0 / cols[j][j : j + 1, :]
            here = row == j
            pivot_row = both[j : j + 1, :] * over
            both = jnp.where(here, pivot_row, both - cols[j] * pivot_row)
            for later in range(j + 1, 8):
                entry = cols[later][j : j + 1, :] * over
                cols[later] = jnp.where(here, entry, cols[later] - cols[j] * entry)
        both = jnp.concatenate([both[8:], both[:8]], axis=0)
        return pltpu.roll(both, LANES - 8, 1)

    both = jnp.concatenate([gram, identity()], axis=1)
    return lax.fori_loop(0, RANK // 8, eliminate, both)[:, :RANK]


def threshold_of(sums, weight):
    count = jnp.sum(sums[0:1, :], axis=1, keepdims=True)
    total = jnp.sum(sums[1:2, :], axis=1, keepdims=True)
    penalty = count / (4.0 * total + 1e-06)
    return penalty, weight / penalty


def left_stack(left):
    first, second = split(left, 2)
    return jnp.concatenate([first, first, second, second], axis=1)


def low_rank(stacked_left, first, second):
    return dot(stacked_left, jnp.concatenate([first, second, first, second], axis=0))


def block_at(half, group):
    return pl.ds(pl.multiple_of(half * 2048 + group * BLOCK, BLOCK), BLOCK)


def join_chunks(chunks, half, group):
    return jnp.concatenate([chunks[half, group, i] for i in range(4)], axis=1)


def factorize(weight, *refs):
    readings, missing, left_in, right_in, seen, clipped, left_out, right_out, sums_out = refs[:9]
    (miss, high, low_part, scaled, right_start, left_start, acc, gram_sum, sums, x_gram, x_gram_in, x_sums,
     x_sums_in, gram_send, gram_core, gram_y, gram_z, partial, from_core, arrived, right_mid, sems, load_sems) = refs[9:]
    used = [0]
    tm = lax.axis_index("tm")
    me = lax.axis_index("sys")
    core = me % 2
    y = (me // 2) % 4
    z = me // 8
    ring = (2, 1, 3)

    def at_sys(z_pos, y_pos, core_pos):
        return {"sys": (z_pos * 4 + y_pos) * 2 + core_pos}

    twin = at_sys(z, y, 1 - core)
    x_dev = {k: {"tm": (tm + k) % 4} for k in ring}
    y_dev = {k: at_sys(z, (y + k) % 4, core) for k in ring}
    z_dev = {k: at_sys((z + k) % 4, y, core) for k in ring}
    plane = {
        (ky, kz): at_sys((z + kz) % 4, (y + ky) % 4, core)
        for ky in range(4) for kz in range(4) if ky or kz
    }

    def send(src, dst, device):
        index = used[0]
        used[0] += 1
        copy = pltpu.make_async_remote_copy(
            src_ref=src, dst_ref=dst, send_sem=sems.at[0, index], recv_sem=sems.at[1, index],
            device_id=device, device_id_type=MESH,
        )
        copy.start()
        return copy

    def load(src, dst, index):
        copy = pltpu.make_async_copy(src, dst, load_sems.at[index])
        copy.start()
        return copy

    small_loads = [load(right_in, right_start, 0), load(left_in, left_start, 1)]
    blocks = [slice(j * BLOCK, (j + 1) * BLOCK) for j in range(8)]
    loads = [
        (load(readings.at[:, at], seen.at[:, at], 2 + 2 * j), load(missing.at[:, at], miss.at[:, at], 3 + 2 * j))
        for j, at in enumerate(blocks)
    ]
    barrier = pltpu.get_barrier_semaphore()
    everyone = list(x_dev.values()) + [twin] + list(plane.values())
    for device in everyone:
        pl.semaphore_signal(barrier, inc=1, device_id=device, device_id_type=MESH)
    for copy in small_loads:
        copy.wait()

    def send_gram(turn, gram):
        x_gram[turn] = fold(gram)
        return [send(x_gram.at[turn], x_gram_in.at[turn, k - 1], x_dev[k]) for k in ring]

    def send_sums(turn):
        return [send(x_sums.at[turn], x_sums_in.at[turn, k - 1], x_dev[k]) for k in ring]

    def finish_gram(turn, copies):
        for copy in copies:
            copy.wait()
        total = (x_gram[turn] + x_gram_in[turn, 0]) + (x_gram_in[turn, 1] + x_gram_in[turn, 2])
        return spd_inverse(unfold(total) + identity())

    def finish_sums(turn, copies):
        for copy in copies:
            copy.wait()
        return (x_sums[turn] + x_sums_in[turn, 0]) + (x_sums_in[turn, 1] + x_sums_in[turn, 2])

    gram = jnp.zeros((RANK, RANK), F32)
    for at in blocks:
        gram += dot_lanes(right_start[:, at], right_start[:, at], HIGH)
    pl.semaphore_wait(barrier, len(everyone))
    gram_copies = send_gram(0, gram)
    stacked_left = left_stack(left_start[...].T)
    acc[...] = jnp.zeros_like(acc)
    sums[...] = jnp.zeros_like(sums)
    for at, copies in zip(blocks, loads):
        right_a, right_b, right_c = split(right_start[:, at], 3)
        low = low_rank(stacked_left, right_a, right_b)
        for copy in copies:
            copy.wait()
        observed = miss[:, at] == 0
        value = seen[:, at]
        seen[:, at] = jnp.where(observed, value, ABSENT)
        target_a, target_b = split(jnp.where(observed, value, low), 2)
        high[:, at] = target_a
        low_part[:, at] = target_b
        acc[...] += dot_lanes(target_a, jnp.concatenate([right_a, right_b, right_c], axis=0))
        acc[:, :LANES] += dot_lanes(target_b, jnp.concatenate([right_a, right_b], axis=0))
        count = jnp.sum(jnp.where(observed, 1.0, 0.0), axis=0, keepdims=True)
        total = jnp.sum(jnp.where(observed, jnp.abs(value), 0.0), axis=0, keepdims=True)
        for piece in range(BLOCK // LANES):
            lanes = slice(piece * LANES, (piece + 1) * LANES)
            sums[0:1, :] += count[:, lanes]
            sums[1:2, :] += total[:, lanes]
    x_sums[0, 0:128, :] = fold(acc[:, :RANK] + acc[:, RANK : 2 * RANK] + acc[:, 2 * RANK :])
    x_sums[0, 128:136, :] = sums[...]
    sum_copies = send_sums(0)
    inverse = finish_gram(0, gram_copies)
    summed = finish_sums(0, sum_copies)
    left = dot_high(unfold(summed[0:128]), inverse)
    left_out[0] = left.T

    def update_right(turn, left, extra, products, finish, target):
        gram_send[turn, 0, 0:32, :] = fold(dot_rows(left, left))
        gram_send[turn, 0, 32:40, :] = extra
        gram_copy = send(gram_send.at[turn, 0], gram_core.at[turn], twin)
        order = (2, 1, 3, 0)
        core_copies = {}
        for ky in order:
            group = (y + ky) % 4
            products(1 - core, group)
            core_copies[ky] = send(partial.at[turn, 1 - core, group], from_core.at[turn, ky], twin)
        gram_copy.wait()
        gram_send[turn, 1] = gram_send[turn, 0] + gram_core[turn]
        y_copies = [send(gram_send.at[turn, 1], gram_y.at[turn, k - 1], y_dev[k]) for k in ring]
        scattered = []
        for ky in order:
            group = (y + ky) % 4
            products(core, group)
            core_copies[ky].wait()
            partial[turn, core, group] += from_core[turn, ky]
            for kz in order:
                if ky or kz:
                    scattered.append(
                        send(partial.at[turn, core, group, (z + kz) % 4], arrived.at[turn, 4 * ky + kz - 1],
                             plane[ky, kz])
                    )
        for copy in y_copies:
            copy.wait()
        gram_send[turn, 2] = (gram_send[turn, 1] + gram_y[turn, 0]) + (gram_y[turn, 1] + gram_y[turn, 2])
        z_copies = [send(gram_send.at[turn, 2], gram_z.at[turn, k - 1], z_dev[k]) for k in ring]
        for copy in z_copies:
            copy.wait()
        grams = (gram_send[turn, 2] + gram_z[turn, 0]) + (gram_z[turn, 1] + gram_z[turn, 2])
        inverse = spd_inverse(unfold(grams[0:32]) + identity())
        finish(grams[32:40])
        for copy in scattered:
            copy.wait()
        total = partial[turn, core, y, z]
        for k in range(0, 15, 3):
            total += (arrived[turn, k] + arrived[turn, k + 1]) + arrived[turn, k + 2]
        target[core, y, z] = dot_high(inverse, total)
        mine = target.at[core, y, z]
        gather = {}
        for ky in order:
            for kz in order:
                if ky or kz:
                    gather[ky, kz] = send(mine, mine, plane[ky, kz])
        near_first = (0, 1, 3, 2)
        to_twin = {}
        for ky in near_first:
            for kz in near_first:
                if ky or kz:
                    gather[ky, kz].wait()
            group = (y + 4 - ky) % 4
            here = target.at[core, group]
            to_twin[ky] = send(here, here, twin)
            yield core, group
        for ky in near_first:
            to_twin[ky].wait()
        for ky in near_first:
            yield 1 - core, (y + 4 - ky) % 4

    def finish_first(total):
        sums_out[...] = total

    stack_a, stack_b, stack_c = split(left.T, 3)
    stacked_two = jnp.concatenate([stack_a, stack_b], axis=0)
    stacked_three = jnp.concatenate([stack_a, stack_b, stack_c], axis=0)

    def products_first(half, group):
        at = block_at(half, group)
        wide = dot(stacked_three, high[:, at])
        small = dot(stacked_two, low_part[:, at])
        value = wide[0:64] + (wide[64:128] + (wide[128:192] + (small[0:64] + small[64:128])))
        for i in range(4):
            partial[0, half, group, i] = value[:, i * LANES : (i + 1) * LANES]

    stacked_left = left_stack(left)
    acc[...] = jnp.zeros_like(acc)
    gram_sum[...] = jnp.zeros_like(gram_sum)
    seen_blocks = 0
    waiting = []
    gram_copies = None

    def middle(half, group):
        _, bound = threshold_of(sums_out[...], weight)
        at = block_at(half, group)
        right_a, right_b = split(join_chunks(right_mid, half, group), 2)
        low = low_rank(stacked_left, right_a, right_b)
        value = seen[:, at]
        inside = jnp.maximum(jnp.minimum(value - low, bound), -bound)
        inside = jnp.where(value < 0.5 * ABSENT, inside, 0.0)
        clipped[:, at] = inside
        ratio = (inside * (1.0 / bound)).astype(BF16)
        scaled[:, at] = ratio
        acc[:, :LANES] += dot_lanes(ratio, jnp.concatenate([right_a, right_b], axis=0))

    for half, group in update_right(0, left, summed[128:136], products_first, finish_first, right_mid):
        cols = join_chunks(right_mid, half, group)
        gram_sum[...] += dot_lanes(cols, cols, HIGH)
        seen_blocks += 1
        if seen_blocks <= 4:
            middle(half, group)
        else:
            waiting.append((half, group))
    gram_copies = send_gram(1, gram_sum[...])
    for half, group in waiting:
        middle(half, group)
    _, bound = threshold_of(sums_out[...], weight)
    scale = (5.0 / 3.0) * bound
    x_sums[1, 0:128, :] = fold((acc[:, :RANK] + acc[:, RANK : 2 * RANK]) * scale)
    x_sums[1, 128:136, :] = jnp.zeros((8, LANES), F32)
    sum_copies = send_sums(1)
    inverse = finish_gram(1, gram_copies)
    summed = finish_sums(1, sum_copies)
    before = left
    left = before + dot_high(unfold(summed[0:128]) - before, inverse)
    left_out[1] = left.T
    mix_a, mix_b, mix_c = split(dot_rows(left, before), 3)
    mixed = jnp.concatenate([mix_a, mix_a, mix_b, mix_c], axis=1)
    last_a, last_b = split(left.T, 2)
    stacked_last = jnp.concatenate([last_a, last_b], axis=0)

    def products_last(half, group):
        at = block_at(half, group)
        wide = dot(stacked_last, scaled[:, at])
        right_a, right_b = split(join_chunks(right_mid, half, group), 2)
        value = dot(mixed, jnp.concatenate([right_a, right_b, right_a, right_a], axis=0))
        value += (wide[0:64] + wide[64:128]) * scale
        for i in range(4):
            partial[1, half, group, i] = value[:, i * LANES : (i + 1) * LANES]

    for _ in update_right(1, left, jnp.zeros((8, LANES), F32), products_last, lambda total: None, right_out):
        pass


def last_pass(weight, seen, clipped, left, right, sums, sparse, dual, right_t, left_t):
    penalty, bound = threshold_of(sums[...], weight)
    cols = jnp.concatenate([right[i] for i in range(BLOCK // LANES)], axis=1)
    right_a, right_b = split(cols, 2)
    low = low_rank(left_stack(left[1].T), right_a, right_b)
    value = seen[...]
    present = value < 0.5 * ABSENT
    shifted = value - low + clipped[...] * (1.0 / 1.5)
    bound = bound / 1.5
    inside = jnp.maximum(jnp.minimum(shifted, bound), -bound)
    sparse[...] = jnp.where(present, shifted - inside, 0.0)
    dual[...] = jnp.where(present, inside * (1.5 * penalty), 0.0)
    right_t[...] = cols
    left_t[...] = left[1]


def params(limit, **more):
    return pltpu.CompilerParams(vmem_limit_bytes=limit * MIB, **more)


def on_device(weight, readings, missing, left_init, right_init):
    rows, times = readings.shape
    steps = times // BLOCK
    shape = jax.ShapeDtypeStruct
    full = shape((rows, times), F32)
    dma = pltpu.SemaphoreType.DMA
    in_vmem = pl.BlockSpec(memory_space=VMEM)
    in_hbm = pl.BlockSpec(memory_space=pltpu.HBM)
    chunked = (2, 4, 4, RANK, LANES)
    seen, clipped, left, right, sums = pl.pallas_call(
        functools.partial(factorize, weight),
        out_shape=[full, full, shape((2, RANK, rows), F32), shape(chunked, F32), shape((8, LANES), F32)],
        in_specs=[in_hbm] * 4,
        out_specs=[in_vmem] * 5,
        scratch_shapes=[
            VMEM((rows, times), jnp.int32),
            VMEM((rows, times), BF16),
            VMEM((rows, times), BF16),
            VMEM((rows, times), BF16),
            VMEM((RANK, times), F32),
            VMEM((RANK, rows), F32),
            VMEM((rows, 3 * RANK), F32),
            VMEM((RANK, RANK), F32),
            VMEM((8, LANES), F32),
            VMEM((2, 32, LANES), F32),
            VMEM((2, 3, 32, LANES), F32),
            VMEM((2, 136, LANES), F32),
            VMEM((2, 3, 136, LANES), F32),
            VMEM((2, 3, 40, LANES), F32),
            VMEM((2, 40, LANES), F32),
            VMEM((2, 3, 40, LANES), F32),
            VMEM((2, 3, 40, LANES), F32),
            VMEM((2,) + chunked, F32),
            VMEM((2, 4, 4, RANK, LANES), F32),
            VMEM((2, 15, RANK, LANES), F32),
            VMEM(chunked, F32),
            dma((2, 102)),
            dma((18,)),
        ],
        compiler_params=params(40, collective_id=0, has_side_effects=True),
    )(readings, missing, left_init.T, right_init.T)
    tile = pl.BlockSpec((rows, BLOCK), lambda i: (0, i))
    fixed = lambda *dims: pl.BlockSpec(dims, lambda i: (0,) * len(dims))
    sparse, dual, right_t, left_t = pl.pallas_call(
        functools.partial(last_pass, weight),
        grid=(steps,),
        out_shape=[full, full, shape((RANK, times), F32), shape((RANK, rows), F32)],
        in_specs=[
            tile, tile, fixed(2, RANK, rows),
            pl.BlockSpec((BLOCK // LANES, RANK, LANES), lambda i: (i, 0, 0)), fixed(8, LANES),
        ],
        out_specs=[tile, tile, pl.BlockSpec((RANK, BLOCK), lambda i: (0, i)), fixed(RANK, rows)],
        compiler_params=params(24),
    )(seen, clipped, left, right.reshape(32, RANK, LANES), sums)
    return left_t.T, right_t.T, sparse, dual


def solution(mesh):
    weight = 1.0 / math.sqrt(max(8192, 16384))
    in_specs = (P("sys", "tm"), P("sys", "tm"), P("sys", None), P("tm", None))
    out_specs = (P("sys", None), P("tm", None), P("sys", "tm"), P("sys", "tm"))
    return jax.shard_map(
        functools.partial(on_device, weight), mesh=mesh, in_specs=in_specs, out_specs=out_specs, check_vma=False
    )
```

time: 532 us -> 86.6 us (0.16)
  blocking collectives: 353 us -> 0 us
  Pallas kernels: 0 us -> 82.4 us
  matrix products: 59.6 us -> 0 us
  other arithmetic: 53.8 us -> 0 us
  waiting for transfers between devices: 37.5 us -> 0 us
  between operations: 17 us -> 0.65 us
    psum x5 -> x0, blocking collectives: 353 us -> none  [the longest x2 253 us: on_device(): gram_u = lax.psum(inner_rows(left_factor, left_factor), 'sys') + identity]
    pallas_call x0 -> x2, Pallas kernels: none -> 82.4 us  [the longest x1 75.3 us: on_device(): pl.pallas_call(functools.partial(factorize, weight), out_shape=[full, ful...]
    dot_general x11 -> x0, matrix products: 50.2 us -> none  [the longest x5 36.3 us: matmul_high(): jnp.dot(first_op, second_op, precision=lax.Precision.HIGHEST, preferred_e...]
    another operation x20 -> x0, other arithmetic: 48.3 us -> none  [the longest x8 22.2 us: ridge_solve(): return jax.scipy.linalg.cho_solve((factor, True), right_side.T).T]
    psum x4 -> x0, waiting for transfers between devices: 37.4 us -> none  [the longest x2 37.4 us: on_device(): left_sums = lax.psum(matmul_high(target, right_factor), 'tm')]
    another operation x8 -> x0, matrix products: 9.36 us -> none  [ridge_solve(): return jax.scipy.linalg.cho_solve((factor, True), right_side.T).T]
    reduce_sum x1 -> x0, other arithmetic: 5.38 us -> none  [on_device(): jnp.sum(observed_mask.astype(jnp.float32))]
  transfers between devices with their start and end apart: 4 -> 0, of which waited for: 2 -> 0; matrix products, arithmetic and copies ran while one was open for 8% -> 0% of each run, Pallas kernels for 0% -> 0%
where the time goes in v2:
time: 86.6 us; the launch traced here: 85.1 us
  Pallas kernels  82.4 us (95%)
  local copies, waits for them, and re-layouts  2.06 us (2%)
    pallas_call x1, Pallas kernels, on_device(): pl.pallas_call(functools.partial(factorize, weight), out_shape=[full, ful...  75.3 us
    pallas_call x1, Pallas kernels, on_device(): pl.pallas_call(functools.partial(last_pass, weight), grid=(steps,), out_s...  7.13 us
    unnamed x4, local copies, waits for them, and re-layouts  2.06 us

profile of v2, /device:TPU:0, one launch (start us, length us, event | category | flops | bytes accessed | tf_op | source)
XLA Modules:
  0.0 85.1 jit_solution(1625308570687869375)
XLA Ops:
  0.6 0.0 copy-start
  0.6 1.2 %copy-done = f32[4096,64]{0,1:T(8,128)S(1)} copy-done((f32[4096,64]{0,1:T(8,128)S(1)}, f32[4096,64]{0,1:T(8,128)}, u32[]{:S(2)}) %copy-start) | copy-done | bytes 1048600
  1.9 0.0 copy-start.1
  1.9 0.8 copy-done.1
  2.7 75.3 %shard_map.75 = (f32[256,4096]{1,0:T(8,128)S(1)}, f32[256,4096]{1,0:T(8,128)S(1)}, f32[2,64,256]{2,1,0:T(8,128)S(1)}, f32[2,4,4,64,128]{4,3,2,1,0:T(8,128)S(1)}, f32[8,128]{1,0:T(8,128)S(1)}) custom-call(f32[256,4096]{1,0:T(8,128)} %refs_0_.1, s32[256,4096]{1,0:T(8,128)} %refs_1_.1, f32[64,256]{1,0:T(8,128)S(1)} %bitcast.7, f32[64,4096]{1,0:T(8,128)S(1)} %bitcast.5), custom_call_target="tpu_custom_call" | custom-call | tf_op jit(solution)/shard_map/pallas_call | solution.py:385
  78.0 7.1 %shard_map.76 = (f32[256,4096]{1,0:T(8,128)}, f32[256,4096]{1,0:T(8,128)}, f32[64,4096]{1,0:T(8,128)}, f32[64,256]{1,0:T(8,128)}) custom-call(f32[256,4096]{1,0:T(8,128)S(1)} %get-tuple-element.13.seen, f32[256,4096]{1,0:T(8,128)S(1)} %get-tuple-element.14.clipped, f32[2,64,256]{2,1,0:T(8,128)S(1)} %get-tuple-element.15.left, f32[32,64,128]{2,1,0:T(8,128)S(1)} %bitcast.6, ...), custom_call_target="tpu_custom_call" | custom-call | tf_op jit(solution)/shard_map/pallas_call | solution.py:419
Async XLA Ops:
  0.6 1.2 %copy-start = (f32[4096,64]{0,1:T(8,128)S(1)}, f32[4096,64]{0,1:T(8,128)}, u32[]{:S(2)}) copy-start(f32[4096,64]{0,1:T(8,128)} %param.7) | copy-start | bytes 3145732
  1.9 0.8 copy-start.1

commit v3 on v2

--- a/solution.py
+++ b/solution.py
@@ -96,6 +96,15 @@
     return penalty, weight / penalty
 
 
+def gram_blocks(stacked):
+    return dot_lanes(stacked, stacked)
+
+
+def sum_blocks(wide):
+    rows = wide[0:64] + (wide[64:128] + wide[128:192])
+    return rows[:, 0:64] + (rows[:, 64:128] + rows[:, 128:192])
+
+
 def left_stack(left):
     first, second = split(left, 2)
     return jnp.concatenate([first, first, second, second], axis=1)
@@ -116,7 +125,7 @@
 def factorize(weight, *refs):
     readings, missing, left_in, right_in, seen, clipped, left_out, right_out, sums_out = refs[:9]
     (miss, high, low_part, scaled, right_start, left_start, acc, gram_sum, sums, x_gram, x_gram_in, x_sums,
-     x_sums_in, gram_send, gram_core, gram_y, gram_z, partial, from_core, arrived, right_mid, sems, load_sems) = refs[9:]
+     x_sums_in, gram_own, gram_core, gram_send, gram_in, gram_total, gram_twin, partial, from_core, arrived, right_mid, sems, load_sems) = refs[9:]
     used = [0]
     tm = lax.axis_index("tm")
     me = lax.axis_index("sys")
@@ -130,8 +139,6 @@
 
     twin = at_sys(z, y, 1 - core)
     x_dev = {k: {"tm": (tm + k) % 4} for k in ring}
-    y_dev = {k: at_sys(z, (y + k) % 4, core) for k in ring}
-    z_dev = {k: at_sys((z + k) % 4, y, core) for k in ring}
     plane = {
         (ky, kz): at_sys((z + kz) % 4, (y + ky) % 4, core)
         for ky in range(4) for kz in range(4) if ky or kz
@@ -183,14 +190,13 @@
             copy.wait()
         return (x_sums[turn] + x_sums_in[turn, 0]) + (x_sums_in[turn, 1] + x_sums_in[turn, 2])
 
-    gram = jnp.zeros((RANK, RANK), F32)
-    for at in blocks:
-        gram += dot_lanes(right_start[:, at], right_start[:, at], HIGH)
-    pl.semaphore_wait(barrier, len(everyone))
-    gram_copies = send_gram(0, gram)
     stacked_left = left_stack(left_start[...].T)
     acc[...] = jnp.zeros_like(acc)
+    gram_sum[...] = jnp.zeros_like(gram_sum)
     sums[...] = jnp.zeros_like(sums)
+    for at in blocks:
+        stacked = jnp.concatenate(split(right_start[:, at], 3), axis=0)
+        gram_sum[...] += gram_blocks(stacked)
     for at, copies in zip(blocks, loads):
         right_a, right_b, right_c = split(right_start[:, at], 3)
         low = low_rank(stacked_left, right_a, right_b)
@@ -210,6 +216,8 @@
             lanes = slice(piece * LANES, (piece + 1) * LANES)
             sums[0:1, :] += count[:, lanes]
             sums[1:2, :] += total[:, lanes]
+    pl.semaphore_wait(barrier, len(everyone))
+    gram_copies = send_gram(0, sum_blocks(gram_sum[...]))
     x_sums[0, 0:128, :] = fold(acc[:, :RANK] + acc[:, RANK : 2 * RANK] + acc[:, 2 * RANK :])
     x_sums[0, 128:136, :] = sums[...]
     sum_copies = send_sums(0)
@@ -218,10 +226,11 @@
     left = dot_high(unfold(summed[0:128]), inverse)
     left_out[0] = left.T
 
-    def update_right(turn, left, extra, products, finish, target):
-        gram_send[turn, 0, 0:32, :] = fold(dot_rows(left, left))
-        gram_send[turn, 0, 32:40, :] = extra
-        gram_copy = send(gram_send.at[turn, 0], gram_core.at[turn], twin)
+    def update_right(turn, left, stacked, extra, products, finish, target, send_order):
+        gram_own[turn] = fold(sum_blocks(gram_blocks(stacked)))
+        theirs = pl.ds(pl.multiple_of(16 * (1 - core), 16), 16)
+        ours = pl.ds(pl.multiple_of(16 * core, 16), 16)
+        gram_copy = send(gram_own.at[turn, theirs], gram_core.at[turn], twin)
         order = (2, 1, 3, 0)
         core_copies = {}
         for ky in order:
@@ -229,8 +238,12 @@
             products(1 - core, group)
             core_copies[ky] = send(partial.at[turn, 1 - core, group], from_core.at[turn, ky], twin)
         gram_copy.wait()
-        gram_send[turn, 1] = gram_send[turn, 0] + gram_core[turn]
-        y_copies = [send(gram_send.at[turn, 1], gram_y.at[turn, k - 1], y_dev[k]) for k in ring]
+        gram_send[turn, 0:16, :] = gram_own[turn, ours, :] + gram_core[turn]
+        gram_send[turn, 16:24, :] = extra
+        gram_copies = [
+            send(gram_send.at[turn], gram_in.at[turn, 4 * ky + kz - 1], plane[ky, kz])
+            for ky in order for kz in order if ky or kz
+        ]
         scattered = []
         for ky in order:
             group = (y + ky) % 4
@@ -243,15 +256,19 @@
                         send(partial.at[turn, core, group, (z + kz) % 4], arrived.at[turn, 4 * ky + kz - 1],
                              plane[ky, kz])
                     )
-        for copy in y_copies:
+        for copy in gram_copies:
             copy.wait()
-        gram_send[turn, 2] = (gram_send[turn, 1] + gram_y[turn, 0]) + (gram_y[turn, 1] + gram_y[turn, 2])
-        z_copies = [send(gram_send.at[turn, 2], gram_z.at[turn, k - 1], z_dev[k]) for k in ring]
-        for copy in z_copies:
-            copy.wait()
-        grams = (gram_send[turn, 2] + gram_z[turn, 0]) + (gram_z[turn, 1] + gram_z[turn, 2])
-        inverse = spd_inverse(unfold(grams[0:32]) + identity())
-        finish(grams[32:40])
+        total = gram_send[turn]
+        for k in range(0, 15, 3):
+            total += (gram_in[turn, k] + gram_in[turn, k + 1]) + gram_in[turn, k + 2]
+        gram_total[turn] = total
+        send(gram_total.at[turn], gram_twin.at[turn], twin).wait()
+        other = gram_twin[turn]
+        folded = jnp.concatenate(
+            [jnp.where(core == 0, total[0:16], other[0:16]), jnp.where(core == 0, other[0:16], total[0:16])], axis=0
+        )
+        inverse = spd_inverse(unfold(folded) + identity())
+        finish(total[16:24] + other[16:24])
         for copy in scattered:
             copy.wait()
         total = partial[turn, core, y, z]
@@ -260,8 +277,8 @@
         target[core, y, z] = dot_high(inverse, total)
         mine = target.at[core, y, z]
         gather = {}
-        for ky in order:
-            for kz in order:
+        for ky in send_order:
+            for kz in send_order:
                 if ky or kz:
                     gather[ky, kz] = send(mine, mine, plane[ky, kz])
         near_first = (0, 1, 3, 2)
@@ -297,6 +314,8 @@
     stacked_left = left_stack(left)
     acc[...] = jnp.zeros_like(acc)
     gram_sum[...] = jnp.zeros_like(gram_sum)
+    near = (0, 1, 3, 2)
+    far = (2, 1, 3, 0)
     seen_blocks = 0
     waiting = []
     gram_copies = None
@@ -314,15 +333,17 @@
         scaled[:, at] = ratio
         acc[:, :LANES] += dot_lanes(ratio, jnp.concatenate([right_a, right_b], axis=0))
 
-    for half, group in update_right(0, left, summed[128:136], products_first, finish_first, right_mid):
-        cols = join_chunks(right_mid, half, group)
-        gram_sum[...] += dot_lanes(cols, cols, HIGH)
+    for half, group in update_right(
+        0, left, stacked_three, summed[128:136], products_first, finish_first, right_mid, near
+    ):
+        stacked = jnp.concatenate(split(join_chunks(right_mid, half, group), 3), axis=0)
+        gram_sum[...] += gram_blocks(stacked)
         seen_blocks += 1
         if seen_blocks <= 4:
             middle(half, group)
         else:
             waiting.append((half, group))
-    gram_copies = send_gram(1, gram_sum[...])
+    gram_copies = send_gram(1, sum_blocks(gram_sum[...]))
     for half, group in waiting:
         middle(half, group)
     _, bound = threshold_of(sums_out[...], weight)
@@ -337,8 +358,8 @@
     left_out[1] = left.T
     mix_a, mix_b, mix_c = split(dot_rows(left, before), 3)
     mixed = jnp.concatenate([mix_a, mix_a, mix_b, mix_c], axis=1)
-    last_a, last_b = split(left.T, 2)
-    stacked_last = jnp.concatenate([last_a, last_b], axis=0)
+    stacked_all = jnp.concatenate(split(left.T, 3), axis=0)
+    stacked_last = stacked_all[0:128]
 
     def products_last(half, group):
         at = block_at(half, group)
@@ -349,24 +370,42 @@
         for i in range(4):
             partial[1, half, group, i] = value[:, i * LANES : (i + 1) * LANES]
 
-    for _ in update_right(1, left, jnp.zeros((8, LANES), F32), products_last, lambda total: None, right_out):
+    for _ in update_right(
+        1, left, stacked_all, jnp.zeros((8, LANES), F32), products_last, lambda total: None, right_out, far
+    ):
         pass
 
 
-def last_pass(weight, seen, clipped, left, right, sums, sparse, dual, right_t, left_t):
+def last_pass(weight, seen, clipped, left, right, sums, sparse, dual, right_t, left_t, sparse_v, dual_v, right_v, sems):
+    used = []
+
+    def store(src, dst):
+        copy = pltpu.make_async_copy(src, dst, sems.at[len(used)])
+        copy.start()
+        used.append(copy)
+
+    store(left.at[1], left_t)
     penalty, bound = threshold_of(sums[...], weight)
-    cols = jnp.concatenate([right[i] for i in range(BLOCK // LANES)], axis=1)
-    right_a, right_b = split(cols, 2)
-    low = low_rank(left_stack(left[1].T), right_a, right_b)
-    value = seen[...]
-    present = value < 0.5 * ABSENT
-    shifted = value - low + clipped[...] * (1.0 / 1.5)
+    penalty = 1.5 * penalty
     bound = bound / 1.5
-    inside = jnp.maximum(jnp.minimum(shifted, bound), -bound)
-    sparse[...] = jnp.where(present, shifted - inside, 0.0)
-    dual[...] = jnp.where(present, inside * (1.5 * penalty), 0.0)
-    right_t[...] = cols
-    left_t[...] = left[1]
+    stacked_left = left_stack(left[1].T)
+    for block in range(8):
+        at = slice(block * BLOCK, (block + 1) * BLOCK)
+        cols = join_chunks(right, block // 4, block % 4)
+        right_v[:, at] = cols
+        store(right_v.at[:, at], right_t.at[:, at])
+        right_a, right_b = split(cols, 2)
+        low = low_rank(stacked_left, right_a, right_b)
+        value = seen[:, at]
+        present = value < 0.5 * ABSENT
+        shifted = value - low + clipped[:, at] * (1.0 / 1.5)
+        inside = jnp.maximum(jnp.minimum(shifted, bound), -bound)
+        sparse_v[:, at] = jnp.where(present, shifted - inside, 0.0)
+        store(sparse_v.at[:, at], sparse.at[:, at])
+        dual_v[:, at] = jnp.where(present, inside * penalty, 0.0)
+        store(dual_v.at[:, at], dual.at[:, at])
+    for copy in used:
+        copy.wait()
 
 
 def params(limit, **more):
@@ -375,7 +414,6 @@
 
 def on_device(weight, readings, missing, left_init, right_init):
     rows, times = readings.shape
-    steps = times // BLOCK
     shape = jax.ShapeDtypeStruct
     full = shape((rows, times), F32)
     dma = pltpu.SemaphoreType.DMA
@@ -395,38 +433,35 @@
             VMEM((RANK, times), F32),
             VMEM((RANK, rows), F32),
             VMEM((rows, 3 * RANK), F32),
-            VMEM((RANK, RANK), F32),
+            VMEM((3 * RANK, 3 * RANK), F32),
             VMEM((8, LANES), F32),
             VMEM((2, 32, LANES), F32),
             VMEM((2, 3, 32, LANES), F32),
             VMEM((2, 136, LANES), F32),
             VMEM((2, 3, 136, LANES), F32),
-            VMEM((2, 3, 40, LANES), F32),
-            VMEM((2, 40, LANES), F32),
-            VMEM((2, 3, 40, LANES), F32),
-            VMEM((2, 3, 40, LANES), F32),
+            VMEM((2, 32, LANES), F32),
+            VMEM((2, 16, LANES), F32),
+            VMEM((2, 24, LANES), F32),
+            VMEM((2, 15, 24, LANES), F32),
+            VMEM((2, 24, LANES), F32),
+            VMEM((2, 24, LANES), F32),
             VMEM((2,) + chunked, F32),
             VMEM((2, 4, 4, RANK, LANES), F32),
             VMEM((2, 15, RANK, LANES), F32),
             VMEM(chunked, F32),
-            dma((2, 102)),
+            dma((2, 122)),
             dma((18,)),
         ],
         compiler_params=params(40, collective_id=0, has_side_effects=True),
-    )(readings, missing, left_init.T, right_init.T)
-    tile = pl.BlockSpec((rows, BLOCK), lambda i: (0, i))
-    fixed = lambda *dims: pl.BlockSpec(dims, lambda i: (0,) * len(dims))
+    )(*(pltpu.with_memory_space_constraint(arg, pltpu.HBM) for arg in (readings, missing, left_init.T, right_init.T)))
     sparse, dual, right_t, left_t = pl.pallas_call(
         functools.partial(last_pass, weight),
-        grid=(steps,),
         out_shape=[full, full, shape((RANK, times), F32), shape((RANK, rows), F32)],
-        in_specs=[
-            tile, tile, fixed(2, RANK, rows),
-            pl.BlockSpec((BLOCK // LANES, RANK, LANES), lambda i: (i, 0, 0)), fixed(8, LANES),
-        ],
-        out_specs=[tile, tile, pl.BlockSpec((RANK, BLOCK), lambda i: (0, i)), fixed(RANK, rows)],
+        in_specs=[in_vmem] * 5,
+        out_specs=[in_hbm] * 4,
+        scratch_shapes=[VMEM((rows, times), F32), VMEM((rows, times), F32), VMEM((RANK, times), F32), dma((25,))],
         compiler_params=params(24),
-    )(seen, clipped, left, right.reshape(32, RANK, LANES), sums)
+    )(seen, clipped, left, right, sums)
     return left_t.T, right_t.T, sparse, dual
 
 

time: 86.6 us -> 78.4 us (0.905)
  Pallas kernels: 82.4 us -> 76.2 us
  local copies, waits for them, and re-layouts: 2.06 us -> 0 us
    pallas_call x1, Pallas kernels: 75.3 us -> 71.7 us  [on_device(): pl.pallas_call(functools.partial(factorize, weight), out_shape=[full, ful...]
    pallas_call x1, Pallas kernels: 7.13 us -> 4.42 us  [on_device(): pl.pallas_call(functools.partial(last_pass, weight), out_shape=[full, ful...]
    unnamed x4 -> x0, local copies, waits for them, and re-layouts: 2.06 us -> none
where the time goes in v3:
time: 78.4 us; the launch traced here: 77 us
  Pallas kernels  76.2 us (97%)
  between operations  0.8 us (1%)
    pallas_call x1, Pallas kernels, on_device(): pl.pallas_call(functools.partial(factorize, weight), out_shape=[full, ful...  71.7 us
    pallas_call x1, Pallas kernels, on_device(): pl.pallas_call(functools.partial(last_pass, weight), out_shape=[full, ful...  4.42 us

profile of v3, /device:TPU:0, one launch (start us, length us, event | category | flops | bytes accessed | tf_op | source)
XLA Modules:
  0.0 77.0 jit_solution(3795292051930916376)
XLA Ops:
  0.6 71.7 %shard_map.75 = (f32[256,4096]{1,0:T(8,128)S(1)}, f32[256,4096]{1,0:T(8,128)S(1)}, f32[2,64,256]{2,1,0:T(8,128)S(1)}, f32[2,4,4,64,128]{4,3,2,1,0:T(8,128)S(1)}, f32[8,128]{1,0:T(8,128)S(1)}) custom-call(f32[256,4096]{1,0:T(8,128)} %refs_0_.1, s32[256,4096]{1,0:T(8,128)} %refs_1_.1, f32[64,256]{1,0:T(8,128)} %bitcast.5, f32[64,4096]{1,0:T(8,128)} %bitcast.4), custom_call_target="tpu_custom_call" | custom-call | tf_op jit(solution)/shard_map/pallas_call | solution.py:423
  72.4 4.4 %shard_map.76 = (f32[256,4096]{1,0:T(8,128)}, f32[256,4096]{1,0:T(8,128)}, f32[64,4096]{1,0:T(8,128)}, f32[64,256]{1,0:T(8,128)}) custom-call(f32[256,4096]{1,0:T(8,128)S(1)} %get-tuple-element.13.seen, f32[256,4096]{1,0:T(8,128)S(1)} %get-tuple-element.14.clipped, f32[2,64,256]{2,1,0:T(8,128)S(1)} %get-tuple-element.15.left, ...), custom_call_target="tpu_custom_call" | custom-call | tf_op jit(solution)/shard_map/pallas_call | solution.py:457

commit v4 on v3

--- a/solution.py
+++ b/solution.py
@@ -18,6 +18,11 @@
 ABSENT = 1e30
 BLOCK = 512
 MIB = 1 << 20
+PARTS = 2
+WIDE = 1024
+NEAR = (0, 1, 3, 2)
+FAR = (2, 1, 3, 0)
+FIRST_ORDER = FAR
 
 
 def split(value, parts):
@@ -105,6 +110,19 @@
     return rows[:, 0:64] + (rows[:, 64:128] + rows[:, 128:192])
 
 
+def solver(inverse):
+    first, second, third = split(inverse, 3)
+    large = jnp.concatenate([first, first, second, second], axis=1)
+    small = jnp.concatenate([first, third], axis=1)
+
+    def solve(cols):
+        col_a, col_b, col_c = split(cols, 3)
+        fine = dot(small, jnp.concatenate([col_c, col_a], axis=0))
+        return fine + dot(large, jnp.concatenate([col_a, col_b, col_a, col_b], axis=0))
+
+    return solve
+
+
 def left_stack(left):
     first, second = split(left, 2)
     return jnp.concatenate([first, first, second, second], axis=1)
@@ -123,9 +141,9 @@
 
 
 def factorize(weight, *refs):
-    readings, missing, left_in, right_in, seen, clipped, left_out, right_out, sums_out = refs[:9]
+    readings, missing, left_in, right_in, seen, clipped, left_out, right_out, sums_out, inverse_out = refs[:10]
     (miss, high, low_part, scaled, right_start, left_start, acc, gram_sum, sums, x_gram, x_gram_in, x_sums,
-     x_sums_in, gram_own, gram_core, gram_send, gram_in, gram_total, gram_twin, partial, from_core, arrived, right_mid, sems, load_sems) = refs[9:]
+     x_sums_in, gram_send, gram_core, gram_y, gram_z, partial, from_core, arrived, right_mid, right_solved, sems, load_sems) = refs[10:]
     used = [0]
     tm = lax.axis_index("tm")
     me = lax.axis_index("sys")
@@ -138,6 +156,8 @@
         return {"sys": (z_pos * 4 + y_pos) * 2 + core_pos}
 
     twin = at_sys(z, y, 1 - core)
+    y_dev = {k: at_sys(z, (y + k) % 4, core) for k in ring}
+    z_dev = {k: at_sys((z + k) % 4, y, core) for k in ring}
     x_dev = {k: {"tm": (tm + k) % 4} for k in ring}
     plane = {
         (ky, kz): at_sys((z + kz) % 4, (y + ky) % 4, core)
@@ -197,7 +217,10 @@
     for at in blocks:
         stacked = jnp.concatenate(split(right_start[:, at], 3), axis=0)
         gram_sum[...] += gram_blocks(stacked)
-    for at, copies in zip(blocks, loads):
+    for block, (at, copies) in enumerate(zip(blocks, loads)):
+        if block == 4:
+            pl.semaphore_wait(barrier, len(everyone))
+            gram_copies = send_gram(0, sum_blocks(gram_sum[...]))
         right_a, right_b, right_c = split(right_start[:, at], 3)
         low = low_rank(stacked_left, right_a, right_b)
         for copy in copies:
@@ -216,8 +239,6 @@
             lanes = slice(piece * LANES, (piece + 1) * LANES)
             sums[0:1, :] += count[:, lanes]
             sums[1:2, :] += total[:, lanes]
-    pl.semaphore_wait(barrier, len(everyone))
-    gram_copies = send_gram(0, sum_blocks(gram_sum[...]))
     x_sums[0, 0:128, :] = fold(acc[:, :RANK] + acc[:, RANK : 2 * RANK] + acc[:, 2 * RANK :])
     x_sums[0, 128:136, :] = sums[...]
     sum_copies = send_sums(0)
@@ -226,11 +247,10 @@
     left = dot_high(unfold(summed[0:128]), inverse)
     left_out[0] = left.T
 
-    def update_right(turn, left, stacked, extra, products, finish, target, send_order):
-        gram_own[turn] = fold(sum_blocks(gram_blocks(stacked)))
-        theirs = pl.ds(pl.multiple_of(16 * (1 - core), 16), 16)
-        ours = pl.ds(pl.multiple_of(16 * core, 16), 16)
-        gram_copy = send(gram_own.at[turn, theirs], gram_core.at[turn], twin)
+    def update_right(turn, stacked, extra, products, finish, target, send_order):
+        gram_send[turn, 0, 0:32, :] = fold(sum_blocks(gram_blocks(stacked)))
+        gram_send[turn, 0, 32:40, :] = extra
+        gram_copy = send(gram_send.at[turn, 0], gram_core.at[turn], twin)
         order = (2, 1, 3, 0)
         core_copies = {}
         for ky in order:
@@ -238,66 +258,68 @@
             products(1 - core, group)
             core_copies[ky] = send(partial.at[turn, 1 - core, group], from_core.at[turn, ky], twin)
         gram_copy.wait()
-        gram_send[turn, 0:16, :] = gram_own[turn, ours, :] + gram_core[turn]
-        gram_send[turn, 16:24, :] = extra
-        gram_copies = [
-            send(gram_send.at[turn], gram_in.at[turn, 4 * ky + kz - 1], plane[ky, kz])
-            for ky in order for kz in order if ky or kz
-        ]
-        scattered = []
+        gram_send[turn, 1] = gram_send[turn, 0] + gram_core[turn]
+        y_copies = [send(gram_send.at[turn, 1], gram_y.at[turn, k - 1], y_dev[k]) for k in ring]
+        parts = [slice(i * RANK // PARTS, (i + 1) * RANK // PARTS) for i in range(PARTS)]
+
+        def scatter(ky, part):
+            group = (y + ky) % 4
+            return [
+                send(partial.at[turn, core, group, (z + kz) % 4, part], arrived.at[turn, 4 * ky + kz - 1, part],
+                     plane[ky, kz])
+                for kz in order if ky or kz
+            ]
+
+        scattered = [[] for _ in parts]
         for ky in order:
             group = (y + ky) % 4
             products(core, group)
             core_copies[ky].wait()
             partial[turn, core, group] += from_core[turn, ky]
-            for kz in order:
-                if ky or kz:
-                    scattered.append(
-                        send(partial.at[turn, core, group, (z + kz) % 4], arrived.at[turn, 4 * ky + kz - 1],
-                             plane[ky, kz])
-                    )
-        for copy in gram_copies:
+            scattered[0] += scatter(ky, parts[0])
+        for part, copies in zip(parts[1:], scattered[1:]):
+            for ky in order:
+                copies += scatter(ky, part)
+        for copy in y_copies:
             copy.wait()
-        total = gram_send[turn]
-        for k in range(0, 15, 3):
-            total += (gram_in[turn, k] + gram_in[turn, k + 1]) + gram_in[turn, k + 2]
-        gram_total[turn] = total
-        send(gram_total.at[turn], gram_twin.at[turn], twin).wait()
-        other = gram_twin[turn]
-        folded = jnp.concatenate(
-            [jnp.where(core == 0, total[0:16], other[0:16]), jnp.where(core == 0, other[0:16], total[0:16])], axis=0
-        )
-        inverse = spd_inverse(unfold(folded) + identity())
-        finish(total[16:24] + other[16:24])
-        for copy in scattered:
+        gram_send[turn, 2] = (gram_send[turn, 1] + gram_y[turn, 0]) + (gram_y[turn, 1] + gram_y[turn, 2])
+        z_copies = [send(gram_send.at[turn, 2], gram_z.at[turn, k - 1], z_dev[k]) for k in ring]
+        mine = target.at[core, y, z]
+        gather = {(ky, kz): [] for ky in range(4) for kz in range(4)}
+        for part, copies in zip(parts, scattered):
+            for copy in copies:
+                copy.wait()
+            total = partial[turn, core, y, z, part]
+            for k in range(0, 15, 3):
+                total += (arrived[turn, k, part] + arrived[turn, k + 1, part]) + arrived[turn, k + 2, part]
+            target[core, y, z, part] = total
+            for ky in send_order:
+                for kz in send_order:
+                    if ky or kz:
+                        gather[ky, kz].append(send(mine.at[part], mine.at[part], plane[ky, kz]))
+        for copy in z_copies:
             copy.wait()
-        total = partial[turn, core, y, z]
-        for k in range(0, 15, 3):
-            total += (arrived[turn, k] + arrived[turn, k + 1]) + arrived[turn, k + 2]
-        target[core, y, z] = dot_high(inverse, total)
-        mine = target.at[core, y, z]
-        gather = {}
-        for ky in send_order:
-            for kz in send_order:
-                if ky or kz:
-                    gather[ky, kz] = send(mine, mine, plane[ky, kz])
+        grams = (gram_send[turn, 2] + gram_z[turn, 0]) + (gram_z[turn, 1] + gram_z[turn, 2])
+        finish(spd_inverse(unfold(grams[0:32]) + identity()), grams[32:40])
         near_first = (0, 1, 3, 2)
         to_twin = {}
         for ky in near_first:
             for kz in near_first:
-                if ky or kz:
-                    gather[ky, kz].wait()
+                for copy in gather[ky, kz]:
+                    copy.wait()
             group = (y + 4 - ky) % 4
             here = target.at[core, group]
             to_twin[ky] = send(here, here, twin)
             yield core, group
         for ky in near_first:
             to_twin[ky].wait()
-        for ky in near_first:
-            yield 1 - core, (y + 4 - ky) % 4
-
-    def finish_first(total):
+
+    def finish_first(inverse, total):
         sums_out[...] = total
+        inverse_out[0] = inverse
+
+    def finish_last(inverse, total):
+        inverse_out[1] = inverse
 
     stack_a, stack_b, stack_c = split(left.T, 3)
     stacked_two = jnp.concatenate([stack_a, stack_b], axis=0)
@@ -314,16 +336,9 @@
     stacked_left = left_stack(left)
     acc[...] = jnp.zeros_like(acc)
     gram_sum[...] = jnp.zeros_like(gram_sum)
-    near = (0, 1, 3, 2)
-    far = (2, 1, 3, 0)
-    seen_blocks = 0
-    waiting = []
-    gram_copies = None
-
-    def middle(half, group):
-        _, bound = threshold_of(sums_out[...], weight)
-        at = block_at(half, group)
-        right_a, right_b = split(join_chunks(right_mid, half, group), 2)
+
+    def middle(at, bound):
+        right_a, right_b = split(right_solved[:, at], 2)
         low = low_rank(stacked_left, right_a, right_b)
         value = seen[:, at]
         inside = jnp.maximum(jnp.minimum(value - low, bound), -bound)
@@ -333,19 +348,25 @@
         scaled[:, at] = ratio
         acc[:, :LANES] += dot_lanes(ratio, jnp.concatenate([right_a, right_b], axis=0))
 
+    def solve_block(half, group, solve):
+        at = block_at(half, group)
+        cols = solve(join_chunks(right_mid, half, group))
+        right_solved[:, at] = cols
+        gram_sum[...] += gram_blocks(jnp.concatenate(split(cols, 3), axis=0))
+        return at
+
     for half, group in update_right(
-        0, left, stacked_three, summed[128:136], products_first, finish_first, right_mid, near
+        0, stacked_three, summed[128:136], products_first, finish_first, right_mid, FIRST_ORDER
     ):
-        stacked = jnp.concatenate(split(join_chunks(right_mid, half, group), 3), axis=0)
-        gram_sum[...] += gram_blocks(stacked)
-        seen_blocks += 1
-        if seen_blocks <= 4:
-            middle(half, group)
-        else:
-            waiting.append((half, group))
+        at = solve_block(half, group, solver(inverse_out[0]))
+        middle(at, threshold_of(sums_out[...], weight)[1])
+    solve = solver(inverse_out[0])
+    for group in range(4):
+        solve_block(1 - core, group, solve)
     gram_copies = send_gram(1, sum_blocks(gram_sum[...]))
-    for half, group in waiting:
-        middle(half, group)
+    for wide in range(2048 // WIDE):
+        at = pl.ds(pl.multiple_of((1 - core) * 2048 + wide * WIDE, WIDE), WIDE)
+        middle(at, threshold_of(sums_out[...], weight)[1])
     _, bound = threshold_of(sums_out[...], weight)
     scale = (5.0 / 3.0) * bound
     x_sums[1, 0:128, :] = fold((acc[:, :RANK] + acc[:, RANK : 2 * RANK]) * scale)
@@ -364,19 +385,20 @@
     def products_last(half, group):
         at = block_at(half, group)
         wide = dot(stacked_last, scaled[:, at])
-        right_a, right_b = split(join_chunks(right_mid, half, group), 2)
+        right_a, right_b = split(right_solved[:, at], 2)
         value = dot(mixed, jnp.concatenate([right_a, right_b, right_a, right_a], axis=0))
         value += (wide[0:64] + wide[64:128]) * scale
         for i in range(4):
             partial[1, half, group, i] = value[:, i * LANES : (i + 1) * LANES]
 
     for _ in update_right(
-        1, left, stacked_all, jnp.zeros((8, LANES), F32), products_last, lambda total: None, right_out, far
+        1, stacked_all, jnp.zeros((8, LANES), F32), products_last, finish_last, right_out, FAR
     ):
         pass
 
 
-def last_pass(weight, seen, clipped, left, right, sums, sparse, dual, right_t, left_t, sparse_v, dual_v, right_v, sems):
+def last_pass(weight, seen, clipped, left, right, sums, inverse, sparse, dual, right_t, left_t, sparse_v, dual_v, right_v,
+              sems):
     used = []
 
     def store(src, dst):
@@ -389,9 +411,10 @@
     penalty = 1.5 * penalty
     bound = bound / 1.5
     stacked_left = left_stack(left[1].T)
+    solve = solver(inverse[1])
     for block in range(8):
         at = slice(block * BLOCK, (block + 1) * BLOCK)
-        cols = join_chunks(right, block // 4, block % 4)
+        cols = solve(join_chunks(right, block // 4, block % 4))
         right_v[:, at] = cols
         store(right_v.at[:, at], right_t.at[:, at])
         right_a, right_b = split(cols, 2)
@@ -420,11 +443,12 @@
     in_vmem = pl.BlockSpec(memory_space=VMEM)
     in_hbm = pl.BlockSpec(memory_space=pltpu.HBM)
     chunked = (2, 4, 4, RANK, LANES)
-    seen, clipped, left, right, sums = pl.pallas_call(
+    seen, clipped, left, right, sums, inverse = pl.pallas_call(
         functools.partial(factorize, weight),
-        out_shape=[full, full, shape((2, RANK, rows), F32), shape(chunked, F32), shape((8, LANES), F32)],
+        out_shape=[full, full, shape((2, RANK, rows), F32), shape(chunked, F32), shape((8, LANES), F32),
+                   shape((2, RANK, RANK), F32)],
         in_specs=[in_hbm] * 4,
-        out_specs=[in_vmem] * 5,
+        out_specs=[in_vmem] * 6,
         scratch_shapes=[
             VMEM((rows, times), jnp.int32),
             VMEM((rows, times), BF16),
@@ -439,17 +463,16 @@
             VMEM((2, 3, 32, LANES), F32),
             VMEM((2, 136, LANES), F32),
             VMEM((2, 3, 136, LANES), F32),
-            VMEM((2, 32, LANES), F32),
-            VMEM((2, 16, LANES), F32),
-            VMEM((2, 24, LANES), F32),
-            VMEM((2, 15, 24, LANES), F32),
-            VMEM((2, 24, LANES), F32),
-            VMEM((2, 24, LANES), F32),
+            VMEM((2, 3, 40, LANES), F32),
+            VMEM((2, 40, LANES), F32),
+            VMEM((2, 3, 40, LANES), F32),
+            VMEM((2, 3, 40, LANES), F32),
             VMEM((2,) + chunked, F32),
             VMEM((2, 4, 4, RANK, LANES), F32),
             VMEM((2, 15, RANK, LANES), F32),
             VMEM(chunked, F32),
-            dma((2, 122)),
+            VMEM((RANK, times), F32),
+            dma((2, 2 * (21 + 30 * PARTS))),
             dma((18,)),
         ],
         compiler_params=params(40, collective_id=0, has_side_effects=True),
@@ -457,11 +480,11 @@
     sparse, dual, right_t, left_t = pl.pallas_call(
         functools.partial(last_pass, weight),
         out_shape=[full, full, shape((RANK, times), F32), shape((RANK, rows), F32)],
-        in_specs=[in_vmem] * 5,
+        in_specs=[in_vmem] * 6,
         out_specs=[in_hbm] * 4,
         scratch_shapes=[VMEM((rows, times), F32), VMEM((rows, times), F32), VMEM((RANK, times), F32), dma((25,))],
         compiler_params=params(24),
-    )(seen, clipped, left, right, sums)
+    )(seen, clipped, left, right, sums, inverse)
     return left_t.T, right_t.T, sparse, dual
 
 

time: 78.4 us -> 72.3 us (0.922)
  Pallas kernels: 76.2 us -> 70.1 us
    pallas_call x1, Pallas kernels: 71.7 us -> 65.7 us  [on_device(): pl.pallas_call(functools.partial(factorize, weight), out_shape=[full, ful...]
where the time goes in v4:
time: 72.3 us; the launch traced here: 70.9 us
  Pallas kernels  70.1 us (97%)
  between operations  0.8 us (1%)
    pallas_call x1, Pallas kernels, on_device(): pl.pallas_call(functools.partial(factorize, weight), out_shape=[full, ful...  65.7 us
    pallas_call x1, Pallas kernels, on_device(): pl.pallas_call(functools.partial(last_pass, weight), out_shape=[full, ful...  4.38 us

profile of v4, /device:TPU:0, one launch (start us, length us, event | category | flops | bytes accessed | tf_op | source)
XLA Modules:
  0.0 70.9 jit_solution(5449532968393324546)
XLA Ops:
  0.6 65.7 %shard_map.75 = (f32[256,4096]{1,0:T(8,128)S(1)}, f32[256,4096]{1,0:T(8,128)S(1)}, f32[2,64,256]{2,1,0:T(8,128)S(1)}, f32[2,4,4,64,128]{4,3,2,1,0:T(8,128)S(1)},...) custom-call(f32[256,4096]{1,0:T(8,128)} %refs_0_.1, s32[256,4096]{1,0:T(8,128)} %refs_1_.1, f32[64,256]{1,0:T(8,128)} %bitcast.5, ...), custom_call_target="tpu_custom_call" | custom-call | tf_op jit(solution)/shard_map/pallas_call | solution.py:446
  66.4 4.4 %shard_map.76 = (f32[256,4096]{1,0:T(8,128)}, f32[256,4096]{1,0:T(8,128)}, f32[64,4096]{1,0:T(8,128)}, f32[64,256]{1,0:T(8,128)}) custom-call(f32[256,4096]{1,0:T(8,128)S(1)} %get-tuple-element.14.seen, f32[256,4096]{1,0:T(8,128)S(1)} %get-tuple-element.15.clipped, f32[2,64,256]{2,1,0:T(8,128)S(1)} %get-tuple-element.16.left, ...), custom_call_target="tpu_custom_call" | custom-call | tf_op jit(solution)/shard_map/pallas_call | solution.py:480

commit v5 on v4

--- a/solution.py
+++ b/solution.py
@@ -20,9 +20,7 @@
 MIB = 1 << 20
 PARTS = 2
 WIDE = 1024
-NEAR = (0, 1, 3, 2)
-FAR = (2, 1, 3, 0)
-FIRST_ORDER = FAR
+MEET = 6
 
 
 def split(value, parts):
@@ -143,7 +141,7 @@
 def factorize(weight, *refs):
     readings, missing, left_in, right_in, seen, clipped, left_out, right_out, sums_out, inverse_out = refs[:10]
     (miss, high, low_part, scaled, right_start, left_start, acc, gram_sum, sums, x_gram, x_gram_in, x_sums,
-     x_sums_in, gram_send, gram_core, gram_y, gram_z, partial, from_core, arrived, right_mid, right_solved, sems, load_sems) = refs[10:]
+     x_sums_in, gram_send, gram_core, gram_y, gram_z, partial, from_core, arrived, right_mid, right_solved, gram_half, sems, load_sems) = refs[10:]
     used = [0]
     tm = lax.axis_index("tm")
     me = lax.axis_index("sys")
@@ -179,21 +177,21 @@
         copy.start()
         return copy
 
+    barrier = pltpu.get_barrier_semaphore()
+    everyone = list(x_dev.values()) + [twin] + list(plane.values())
+    for device in everyone:
+        pl.semaphore_signal(barrier, inc=1, device_id=device, device_id_type=MESH)
     small_loads = [load(right_in, right_start, 0), load(left_in, left_start, 1)]
     blocks = [slice(j * BLOCK, (j + 1) * BLOCK) for j in range(8)]
     loads = [
         (load(readings.at[:, at], seen.at[:, at], 2 + 2 * j), load(missing.at[:, at], miss.at[:, at], 3 + 2 * j))
         for j, at in enumerate(blocks)
     ]
-    barrier = pltpu.get_barrier_semaphore()
-    everyone = list(x_dev.values()) + [twin] + list(plane.values())
-    for device in everyone:
-        pl.semaphore_signal(barrier, inc=1, device_id=device, device_id_type=MESH)
     for copy in small_loads:
         copy.wait()
 
-    def send_gram(turn, gram):
-        x_gram[turn] = fold(gram)
+    def send_gram(turn, folded):
+        x_gram[turn] = folded
         return [send(x_gram.at[turn], x_gram_in.at[turn, k - 1], x_dev[k]) for k in ring]
 
     def send_sums(turn):
@@ -218,9 +216,9 @@
         stacked = jnp.concatenate(split(right_start[:, at], 3), axis=0)
         gram_sum[...] += gram_blocks(stacked)
     for block, (at, copies) in enumerate(zip(blocks, loads)):
-        if block == 4:
+        if block == MEET:
             pl.semaphore_wait(barrier, len(everyone))
-            gram_copies = send_gram(0, sum_blocks(gram_sum[...]))
+            gram_copies = send_gram(0, fold(sum_blocks(gram_sum[...])))
         right_a, right_b, right_c = split(right_start[:, at], 3)
         low = low_rank(stacked_left, right_a, right_b)
         for copy in copies:
@@ -247,7 +245,7 @@
     left = dot_high(unfold(summed[0:128]), inverse)
     left_out[0] = left.T
 
-    def update_right(turn, stacked, extra, products, finish, target, send_order):
+    def update_right(turn, stacked, extra, products, finish, target, ready, between):
         gram_send[turn, 0, 0:32, :] = fold(sum_blocks(gram_blocks(stacked)))
         gram_send[turn, 0, 32:40, :] = extra
         gram_copy = send(gram_send.at[turn, 0], gram_core.at[turn], twin)
@@ -293,8 +291,8 @@
             for k in range(0, 15, 3):
                 total += (arrived[turn, k, part] + arrived[turn, k + 1, part]) + arrived[turn, k + 2, part]
             target[core, y, z, part] = total
-            for ky in send_order:
-                for kz in send_order:
+            for ky in order:
+                for kz in order:
                     if ky or kz:
                         gather[ky, kz].append(send(mine.at[part], mine.at[part], plane[ky, kz]))
         for copy in z_copies:
@@ -307,10 +305,9 @@
             for kz in near_first:
                 for copy in gather[ky, kz]:
                     copy.wait()
-            group = (y + 4 - ky) % 4
-            here = target.at[core, group]
+            here = ready((y + 4 - ky) % 4)
             to_twin[ky] = send(here, here, twin)
-            yield core, group
+        between()
         for ky in near_first:
             to_twin[ky].wait()
 
@@ -348,25 +345,31 @@
         scaled[:, at] = ratio
         acc[:, :LANES] += dot_lanes(ratio, jnp.concatenate([right_a, right_b], axis=0))
 
-    def solve_block(half, group, solve):
-        at = block_at(half, group)
-        cols = solve(join_chunks(right_mid, half, group))
+    def middle_half(half):
+        for wide in range(2048 // WIDE):
+            at = pl.ds(pl.multiple_of(half * 2048 + wide * WIDE, WIDE), WIDE)
+            middle(at, threshold_of(sums_out[...], weight)[1])
+
+    def solve_block(group):
+        at = block_at(core, group)
+        cols = solver(inverse_out[0])(join_chunks(right_mid, core, group))
         right_solved[:, at] = cols
         gram_sum[...] += gram_blocks(jnp.concatenate(split(cols, 3), axis=0))
-        return at
-
-    for half, group in update_right(
-        0, stacked_three, summed[128:136], products_first, finish_first, right_mid, FIRST_ORDER
-    ):
-        at = solve_block(half, group, solver(inverse_out[0]))
-        middle(at, threshold_of(sums_out[...], weight)[1])
-    solve = solver(inverse_out[0])
-    for group in range(4):
-        solve_block(1 - core, group, solve)
-    gram_copies = send_gram(1, sum_blocks(gram_sum[...]))
-    for wide in range(2048 // WIDE):
-        at = pl.ds(pl.multiple_of((1 - core) * 2048 + wide * WIDE, WIDE), WIDE)
-        middle(at, threshold_of(sums_out[...], weight)[1])
+        return right_solved.at[:, at]
+
+    gram_copies = []
+
+    def own_half():
+        gram_half[0] = fold(sum_blocks(gram_sum[...]))
+        copy = send(gram_half.at[0], gram_half.at[1], twin)
+        middle_half(core)
+        copy.wait()
+        gram_copies.extend(send_gram(1, gram_half[0] + gram_half[1]))
+
+    update_right(
+        0, stacked_three, summed[128:136], products_first, finish_first, right_mid, solve_block, own_half
+    )
+    middle_half(1 - core)
     _, bound = threshold_of(sums_out[...], weight)
     scale = (5.0 / 3.0) * bound
     x_sums[1, 0:128, :] = fold((acc[:, :RANK] + acc[:, RANK : 2 * RANK]) * scale)
@@ -391,10 +394,10 @@
         for i in range(4):
             partial[1, half, group, i] = value[:, i * LANES : (i + 1) * LANES]
 
-    for _ in update_right(
-        1, stacked_all, jnp.zeros((8, LANES), F32), products_last, finish_last, right_out, FAR
-    ):
-        pass
+    update_right(
+        1, stacked_all, jnp.zeros((8, LANES), F32), products_last, finish_last, right_out,
+        lambda group: right_out.at[core, group], lambda: None,
+    )
 
 
 def last_pass(weight, seen, clipped, left, right, sums, inverse, sparse, dual, right_t, left_t, sparse_v, dual_v, right_v,
@@ -472,7 +475,8 @@
             VMEM((2, 15, RANK, LANES), F32),
             VMEM(chunked, F32),
             VMEM((RANK, times), F32),
-            dma((2, 2 * (21 + 30 * PARTS))),
+            VMEM((2, 32, LANES), F32),
+            dma((2, 43 + 60 * PARTS)),
             dma((18,)),
         ],
         compiler_params=params(40, collective_id=0, has_side_effects=True),

time: 72.3 us -> 71.8 us (level)
  no operation moved by 1% of the time
where the time goes in v5:
time: 71.8 us; the launch traced here: 70.4 us
  Pallas kernels  69.6 us (97%)
  between operations  0.8 us (1%)
    pallas_call x1, Pallas kernels, on_device(): pl.pallas_call(functools.partial(factorize, weight), out_shape=[full, ful...  65.2 us
    pallas_call x1, Pallas kernels, on_device(): pl.pallas_call(functools.partial(last_pass, weight), out_shape=[full, ful...  4.38 us

profile of v5, /device:TPU:0, one launch (start us, length us, event | category | flops | bytes accessed | tf_op | source)
XLA Modules:
  0.0 70.4 jit_solution(16229194868868273606)
XLA Ops:
  0.6 65.2 %shard_map.75 = (f32[256,4096]{1,0:T(8,128)S(1)}, f32[256,4096]{1,0:T(8,128)S(1)}, f32[2,64,256]{2,1,0:T(8,128)S(1)}, f32[2,4,4,64,128]{4,3,2,1,0:T(8,128)S(1)},...) custom-call(f32[256,4096]{1,0:T(8,128)} %refs_0_.1, s32[256,4096]{1,0:T(8,128)} %refs_1_.1, f32[64,256]{1,0:T(8,128)} %bitcast.5, ...), custom_call_target="tpu_custom_call" | custom-call | tf_op jit(solution)/shard_map/pallas_call | solution.py:449
  65.9 4.4 %shard_map.76 = (f32[256,4096]{1,0:T(8,128)}, f32[256,4096]{1,0:T(8,128)}, f32[64,4096]{1,0:T(8,128)}, f32[64,256]{1,0:T(8,128)}) custom-call(f32[256,4096]{1,0:T(8,128)S(1)} %get-tuple-element.14.seen, f32[256,4096]{1,0:T(8,128)S(1)} %get-tuple-element.15.clipped, f32[2,64,256]{2,1,0:T(8,128)S(1)} %get-tuple-element.16.left, ...), custom_call_target="tpu_custom_call" | custom-call | tf_op jit(solution)/shard_map/pallas_call | solution.py:484

commit v6 on v5

--- a/solution.py
+++ b/solution.py
@@ -20,7 +20,7 @@
 MIB = 1 << 20
 PARTS = 2
 WIDE = 1024
-MEET = 6
+MEET = 5
 
 
 def split(value, parts):
@@ -417,10 +417,11 @@
     solve = solver(inverse[1])
     for block in range(8):
         at = slice(block * BLOCK, (block + 1) * BLOCK)
-        cols = solve(join_chunks(right, block // 4, block % 4))
-        right_v[:, at] = cols
+        right_v[:, at] = solve(join_chunks(right, block // 4, block % 4))
         store(right_v.at[:, at], right_t.at[:, at])
-        right_a, right_b = split(cols, 2)
+    for block in range(8):
+        at = slice(block * BLOCK, (block + 1) * BLOCK)
+        right_a, right_b = split(right_v[:, at], 2)
         low = low_rank(stacked_left, right_a, right_b)
         value = seen[:, at]
         present = value < 0.5 * ABSENT

time: 71.8 us -> 71.8 us (level)
  no operation moved by 1% of the time
where the time goes in v6:
time: 71.8 us; the launch traced here: 70.4 us
  Pallas kernels  69.6 us (97%)
  between operations  0.8 us (1%)
    pallas_call x1, Pallas kernels, on_device(): pl.pallas_call(functools.partial(factorize, weight), out_shape=[full, ful...  65.2 us
    pallas_call x1, Pallas kernels, on_device(): pl.pallas_call(functools.partial(last_pass, weight), out_shape=[full, ful...  4.43 us

profile of v6, /device:TPU:0, one launch (start us, length us, event | category | flops | bytes accessed | tf_op | source)
XLA Modules:
  0.0 70.4 jit_solution(284764753887253496)
XLA Ops:
  0.6 65.2 %shard_map.75 = (f32[256,4096]{1,0:T(8,128)S(1)}, f32[256,4096]{1,0:T(8,128)S(1)}, f32[2,64,256]{2,1,0:T(8,128)S(1)}, f32[2,4,4,64,128]{4,3,2,1,0:T(8,128)S(1)},...) custom-call(f32[256,4096]{1,0:T(8,128)} %refs_0_.1, s32[256,4096]{1,0:T(8,128)} %refs_1_.1, f32[64,256]{1,0:T(8,128)} %bitcast.5, ...), custom_call_target="tpu_custom_call" | custom-call | tf_op jit(solution)/shard_map/pallas_call | solution.py:450
  65.8 4.4 %shard_map.76 = (f32[256,4096]{1,0:T(8,128)}, f32[256,4096]{1,0:T(8,128)}, f32[64,4096]{1,0:T(8,128)}, f32[64,256]{1,0:T(8,128)}) custom-call(f32[256,4096]{1,0:T(8,128)S(1)} %get-tuple-element.14.seen, f32[256,4096]{1,0:T(8,128)S(1)} %get-tuple-element.15.clipped, f32[2,64,256]{2,1,0:T(8,128)S(1)} %get-tuple-element.16.left, ...), custom_call_target="tpu_custom_call" | custom-call | tf_op jit(solution)/shard_map/pallas_call | solution.py:485
